TPU v7x, 128 devices: a whole 4x4x4 slice. The times are simulated.
128 devices in a mesh: orient: 16 (over x, y), frame: 8 (over z, core).
Axes of the slice: x: 4, y: 4, z: 4, core: 2. Of those that a mesh axis runs over, the one named last changes fastest.
Arguments:
- counts: int32 [4096, 16384], P(('orient', 'frame')), may hold values from 0 to 8191, as said below
- pixel_gain: float32 [16384], replicated, may hold values from 0.5 to 2
- slices: bfloat16 [8192, 16384], P('orient'), may hold values from 0.25 to 8
- voxel_index: int32 [8192, 128], P('orient'), may hold values from 0 to 6143
- interp: float32 [8192, 128], P('orient'), may hold values from 0.1 to 1
Outputs:
- model: float32 [6144, 128], P(('orient', 'frame'))
Inputs may be any that keep to these rules, and one draw needn't show every extreme that they name: In each frame the counts lie below 2 to the power of a level of the frame's own between 6 and 13; the first frame's level is 13 and its first pixel holds 8191.
All inputs are finite; a program needn't handle non-finite values.
Results may differ from a plain program's by a relative error of at most 0.012.
Values may be sent and summed in bfloat16 or wider, within the bound.
A program may use at most 192 MiB of HBM per device.

v0:
```python
import jax
import jax.numpy as jnp
from jax import lax
from jax.sharding import PartitionSpec as P

VB_DEV = 48


score_beta = 1.5


def local(counts, pixel_gain, slices, voxel_index, interp):
    frames = (counts.astype(jnp.float32) * pixel_gain[None, :]).astype(jnp.bfloat16)
    gathered_rows = lax.all_gather(frames, "orient", axis=0, tiled=True)
    pixel_count = slices.shape[1]
    orient_count = slices.shape[0]
    pixel_blocks = pixel_count // 128
    photons = jnp.sum(gathered_rows, axis=1, dtype=jnp.float32)
    log_slices = jnp.log(slices.astype(jnp.float32)).astype(jnp.bfloat16)
    log_mean = jnp.log(jnp.sum(slices, axis=1, dtype=jnp.float32) / pixel_count)
    score_scale = score_beta / pixel_count
    products = lax.dot_general(
        gathered_rows, log_slices, (((1,), (1,)), ((), ())), preferred_element_type=jnp.float32
    )
    scores = (products - photons[:, None] * log_mean[None, :]) * score_scale
    frame_peak = lax.pmax(jnp.max(scores, axis=1), "orient")
    shifted = jnp.exp(scores - frame_peak[:, None])
    frame_total = lax.psum(jnp.sum(shifted, axis=1), "orient")
    probability = shifted / frame_total[:, None]
    prob_bf = probability.astype(jnp.bfloat16)
    level = photons / pixel_count
    orient_mass = lax.psum(jnp.sum(probability * level[:, None], axis=0), "frame")
    gathered = lax.dot_general(
        prob_bf, gathered_rows, (((0,), (0,)), ((), ())), preferred_element_type=jnp.float32
    )
    prior_share = (lax.axis_index("frame") == 0).astype(jnp.float32)
    denominator = orient_mass + 0.25
    updated = (gathered + 0.25 * prior_share * slices.astype(jnp.float32)) / denominator[:, None]
    weighted = updated.reshape(orient_count, pixel_blocks, 128) * interp[:, :, None]
    orient_size = lax.axis_size("orient")
    frame_size = lax.axis_size("frame")
    voxel_blocks = VB_DEV * orient_size * frame_size
    flat_target = voxel_index.reshape(-1)
    voxel_sum = jax.ops.segment_sum(
        weighted.reshape(-1, 128), flat_target, num_segments=voxel_blocks
    )
    voxel_weight = jax.ops.segment_sum(
        (interp * prior_share).reshape(-1), flat_target, num_segments=voxel_blocks
    )
    summed, weight_sum = (
        lax.psum_scatter(voxel_sum, ("orient", "frame"), scatter_dimension=0, tiled=True),
        lax.psum_scatter(voxel_weight, ("orient", "frame"), scatter_dimension=0, tiled=True),
    )
    return summed / (1.0 + weight_sum)[:, None]


def solution(mesh):
    placed = (
        P(("orient", "frame"), None),
        P(),
        P("orient", None),
        P("orient", None),
        P("orient", None),
    )
    return jax.shard_map(
        local, mesh=mesh, in_specs=placed, out_specs=P(("orient", "frame"), None), check_vma=False
    )
```

profile of v0, /device:TPU:0, one launch (start us, length us, event | category | flops | bytes accessed | tf_op | source)
XLA Modules:
  0.0 1092.5 jit_solution(560090229176393495)
XLA Ops:
  6.5 0.0 all-gather.2.cloned.1.call-start
  6.5 2.8 multiply_convert_fusion
  9.3 0.0 all-gather.2.cloned.1.call-update
  9.3 0.0 reduce-scatter.2.cloned.1.call-start
  9.4 6.9 convert_reduce_fusion
  16.2 106.9 %all-gather.2.cloned.1.call-done = bf16[512,16384]{1,0:T(8,128)(2,1)} async-done(((bf16[32,16384]{1,0:T(8,128)(2,1)}), bf16[512,16384]{1,0:T(8,128)(2,1)}) %all-gather.2.cloned.1.call-update) | async-done | bytes 16777232 | tf_op jit(solution)/shard_map/all_gather | solution.py:14
  123.2 6.8 convert_reduce_fusion.1
  130.1 17.3 %fusion.21 = (f32[512]{0:T(512)S(1)}, f32[512,512]{0,1:T(8,128)S(1)}) fusion(f32[512]{0:T(512)S(1)} %multiply_log_fusion, f32[512]{0:T(512)S(1)} %convert_reduce_fusion.1, bf16[512,16384]{1,0:T(8,128)(2,1)} %all-gather.2.cloned.1.call-done, bf16[512,16384]{1,0:T(8,128)(2,1)} %param.7), kind=kOutput, calls=%fused_computation.30 | convolution fusion | flops 8607760384 | bytes 34609152 | tf_op jit(solution)/shard_map/dot_general | solution.py:22
  147.3 38.4 %pmax.7 = f32[512]{0:T(512)S(1)} all-reduce(f32[512]{0:T(512)S(1)} %get-tuple-element.5), channel_id=1, replica_groups=mesh['orient'=16,'frame'=8] {'orient'}, use_global_device_ids=true, to_apply=%region_3.0 | all-reduce | flops 512 | bytes 4096 | tf_op jit(solution)/shard_map/pmax | solution.py:26
  185.8 0.2 fusion.16
  186.0 35.5 %psum.14 = f32[512]{0:T(512)S(1)} all-reduce(f32[512]{0:T(512)S(1)} %fusion.16), channel_id=1, replica_groups=mesh['orient'=16,'frame'=8] {'orient'}, use_global_device_ids=true, to_apply=%region_5.0 | all-reduce | flops 512 | bytes 4096 | tf_op jit(solution)/shard_map/psum | solution.py:28
  221.4 0.3 multiply_reduce_fusion
  221.7 12.6 %psum.15 = f32[512]{0:T(512)S(1)} all-reduce(f32[512]{0:T(512)S(1)} %multiply_reduce_fusion), channel_id=1, replica_groups=mesh['orient'=16,'frame'=8] {'frame'}, use_global_device_ids=true, to_apply=%region_7.0 | all-reduce | flops 512 | bytes 4096 | tf_op jit(solution)/shard_map/psum | solution.py:32
  234.3 25.7 %fusion.2 = f32[512,16384]{1,0:T(8,128)} fusion(bf16[512,16384]{1,0:T(8,128)(2,1)} %param.7, bf16[512,16384]{1,0:T(8,128)(2,1)} %all-gather.2.cloned.1.call-done, f32[512]{0:T(512)S(1)} %broadcast_add_fusion, f32[]{:T(128)S(6)} %mul.68, f32[512,512]{0,1:T(8,128)S(1)} %get-tuple-element.6, f32[512]{0:T(512)S(1)} %psum.14, f32[512]{0:T(512)S(1)} %pmax.7), kind=kOutput, calls=%fused_computation.7 | convolution fusion | flops 8624275456 | bytes 68163584 | tf_op jit(solution)/shard_map/dot_general | solution.py:33
  260.0 0.0 copy-start
  260.0 35.5 %reshape.24 = f32[65536,128]{1,0:T(8,128)} reshape(f32[512,16384]{1,0:T(8,128)} %fusion.2) | data formatting | bytes 67108864 | tf_op jit(solution)/shard_map/reshape | solution.py:39
  295.5 0.0 copy-done
  295.5 383.0 %scatter_custom_fusion = f32[6144,128]{1,0:T(8,128)} fusion(s32[65536]{0:T(1024)} %bitcast.7, f32[65536,128]{1,0:T(8,128)} %reshape.24, f32[65536]{0:T(1024)S(1)} %bitcast.6, f32[]{:T(128)} %constant.8.clone.1), kind=kCustom, calls=%fused_computation.8 | custom fusion | flops 16777216 | bytes 36962816 | tf_op jit(solution)/shard_map/scatter-add | solution.py:44
  678.5 0.0 reduce-scatter.2.cloned.1.call-update
  678.6 341.8 %scatter_custom_fusion.1 = f32[6144]{0:T(1024)S(1)} fusion(s32[65536]{0:T(1024)} %bitcast.8, f32[65536]{0:T(1024)S(1)} %multiply_bitcast_fusion, f32[]{:T(128)} %constant.8.clone.1), kind=kCustom, calls=%fused_computation.24 | custom fusion | flops 65536 | bytes 25088 | tf_op jit(solution)/shard_map/scatter-add | solution.py:47
  1020.4 63.8 %all-reduce = f32[6144]{0:T(1024)S(1)} all-reduce(f32[6144]{0:T(1024)S(1)} %scatter_custom_fusion.1), channel_id=3, replica_groups=mesh['orient'=16,'frame'=8] {'orient','frame'}, use_global_device_ids=true, to_apply=%region_11.0.clone | all-reduce | flops 6144 | bytes 49152
  1084.1 0.1 dynamic-slice_add_fusion
  1084.2 0.0 reduce-scatter.2.cloned.1.call-done
  1084.2 1.4 broadcast_divide_fusion
  (4 shorter events, 0.0 us)
Async XLA Ops:
  6.5 116.7 %all-gather.2.cloned.1.call-start = ((), (), s32[]{:S(2)}) async-start(), calls=%async_computation.1 | async-start | bytes 17825792 | tf_op jit(solution)/shard_map/all_gather | solution.py:14
  9.3 1074.9 %reduce-scatter.2.cloned.1.call-start = ((), (), s32[]{:S(2)}) async-start(), calls=%async_computation.2 | async-start | bytes 3170304 | tf_op jit(solution)/shard_map/reduce_scatter | solution.py:51
  260.0 35.5 %copy-start = (f32[512,128]{1,0:T(8,128)S(1)}, f32[512,128]{1,0:T(8,128)}, u32[]{:S(2)}) copy-start(f32[512,128]{1,0:T(8,128)} %param.9) | copy-start | bytes 786436
Sparse Core Ops, SparseCore 0:
  9.5 113.6 all-gather.1
  678.7 205.3 reduce-scatter.1
where the time goes:
time: 1090 us
  other arithmetic  743 us (68%)
  blocking collectives  150 us (14%)
  waiting for transfers between devices  107 us (10%)
  matrix products  43 us (4%)
  local copies, waits for them, and re-layouts  35.5 us (3%)
  between operations  13.5 us (1%)
    scatter-add x1, other arithmetic, local(): jax.ops.segment_sum(weighted.reshape(-1, 128), flat_target, num_segments=...  383 us
    scatter-add x1, other arithmetic, local(): jax.ops.segment_sum((interp * prior_share).reshape(-1), flat_target, num_...  342 us
    all_gather x1, waiting for transfers between devices, local(): gathered_rows = lax.all_gather(frames, 'orient', axis=0, tiled=True)  107 us
    unnamed x1, blocking collectives  63.8 us
    pmax x1, blocking collectives, local(): frame_peak = lax.pmax(jnp.max(scores, axis=1), 'orient')  38.4 us
    reshape x1, local copies, waits for them, and re-layouts, local(): updated.reshape(orient_count, pixel_blocks, 128) * interp[:, :, None]  35.5 us
    psum x1, blocking collectives, local(): frame_total = lax.psum(jnp.sum(shifted, axis=1), 'orient')  35.5 us
    dot_general x1, matrix products, local(): lax.dot_general(prob_bf, gathered_rows, (((0,), (0,)), ((), ())), preferr...  25.7 us
  transfers between devices with their start and end apart: 2, of which 1 were waited for; matrix products, arithmetic and copies ran while one was open for 32% of the time, Pallas kernels for 0%

commit v1 on v0

v1 whole, which is shorter than its diff:
```python
import functools

import jax
import jax.numpy as jnp
from jax import lax
from jax.experimental import pallas as pl
from jax.experimental.pallas import tpu as pltpu
from jax.sharding import PartitionSpec as P

VB_DEV = 48
ACCS = 4

score_beta = 1.5


def scatter_kernel(q_count, block_ref, rows_ref, index_hbm, out_ref, index_smem, sem, *accs):
    copy = pltpu.make_async_copy(index_hbm, index_smem, sem)
    copy.start()
    voxels = out_ref.shape[0]
    orients = rows_ref.shape[1]

    def clear(t, carry):
        for acc in accs:
            acc[pl.ds(pl.multiple_of(t * 64, 64), 64), :] = jnp.zeros((64, 128), jnp.float32)
        return carry

    lax.fori_loop(0, voxels // 64, clear, 0)
    copy.wait()
    base = block_ref[0] * q_count

    def step(t, carry):
        n = 0
        for q in range(q_count):
            for s in range(8):
                r = t * 8 + s
                i = index_smem[r, base + q]
                acc = accs[n % len(accs)]
                n += 1
                acc[pl.ds(i, 1), :] += rows_ref[q, pl.ds(r, 1), :]
        return carry

    lax.fori_loop(0, orients // 8, step, 0)

    def finish(t, carry):
        d = pl.ds(pl.multiple_of(t * 64, 64), 64)
        total = accs[0][d, :]
        for acc in accs[1:]:
            total = total + acc[d, :]
        out_ref[d, :] = total
        return carry

    lax.fori_loop(0, voxels // 64, finish, 0)


def scatter(rows, index, block, voxels):
    q_count = rows.shape[0]
    return pl.pallas_call(
        functools.partial(scatter_kernel, q_count),
        out_shape=jax.ShapeDtypeStruct((voxels, 128), jnp.float32),
        in_specs=[
            pl.BlockSpec(memory_space=pltpu.SMEM),
            pl.BlockSpec(memory_space=pltpu.VMEM),
            pl.BlockSpec(memory_space=pl.ANY),
        ],
        out_specs=pl.BlockSpec(memory_space=pltpu.VMEM),
        scratch_shapes=[pltpu.SMEM(index.shape, jnp.int32), pltpu.SemaphoreType.DMA]
        + [pltpu.VMEM((voxels, 128), jnp.float32)] * ACCS,
        compiler_params=pltpu.CompilerParams(vmem_limit_bytes=48 * 2**20),
    )(block, rows, index)


def local(counts, pixel_gain, slices, voxel_index, interp):
    frame_size = lax.axis_size("frame")
    orient_size = lax.axis_size("orient")
    me = lax.axis_index("frame")
    pixel_count = slices.shape[1]
    orient_count = slices.shape[0]
    part = pixel_count // frame_size
    q_count = part // 128
    voxels = VB_DEV * orient_size * frame_size
    own = (counts.astype(jnp.float32) * pixel_gain[None, :]).astype(jnp.bfloat16)
    column = lax.all_to_all(own, "frame", split_axis=1, concat_axis=0, tiled=True)
    frames = lax.all_gather(column, "orient", axis=0, tiled=True)
    log_mean = jnp.log(jnp.sum(slices, axis=1, dtype=jnp.float32) / pixel_count)
    slice_part = lax.dynamic_slice_in_dim(slices, me * part, part, axis=1).astype(jnp.float32)
    log_slices = jnp.log(slice_part).astype(jnp.bfloat16)
    photons_part = jnp.sum(frames, axis=1, dtype=jnp.float32)
    score_scale = score_beta / pixel_count
    products = lax.dot_general(
        frames, log_slices, (((1,), (1,)), ((), ())), preferred_element_type=jnp.float32
    )
    partial = (products - photons_part[:, None] * log_mean[None, :]) * score_scale
    scores = lax.psum_scatter(partial, "frame", scatter_dimension=0, tiled=True)
    photons = lax.psum_scatter(photons_part, "frame", scatter_dimension=0, tiled=True)
    frame_peak = lax.pmax(jnp.max(scores, axis=1), "orient")
    shifted = jnp.exp(scores - frame_peak[:, None])
    frame_total = lax.psum(jnp.sum(shifted, axis=1), "orient")
    probability = shifted / frame_total[:, None]
    mass = lax.psum(jnp.sum(probability * (photons / pixel_count)[:, None], axis=0), "frame")
    prob = lax.all_gather(probability.astype(jnp.bfloat16), "frame", axis=0, tiled=True)
    gathered = lax.dot_general(
        prob, frames, (((0,), (0,)), ((), ())), preferred_element_type=jnp.float32
    )
    index = voxel_index
    weight = lax.dynamic_slice_in_dim(interp, me * q_count, q_count, axis=1)
    share = weight / (mass + 0.25)[:, None]
    rows = (gathered + 0.25 * slice_part).reshape(orient_count, q_count, 128).transpose(1, 0, 2)
    rows = rows * share.T[:, :, None]
    block = jnp.full((1,), me, jnp.int32)
    voxel_sum = scatter(rows, index, block, voxels)
    targets = lax.dynamic_slice_in_dim(voxel_index, me * q_count, q_count, axis=1).reshape(1, -1)
    flat_weight = weight.reshape(1, -1)
    upper, lower = targets // VB_DEV, targets % VB_DEV
    hot_upper = (upper == lax.broadcasted_iota(jnp.int32, (128, 1), 0)).astype(jnp.float32)
    hot_lower = jnp.where(lower == lax.broadcasted_iota(jnp.int32, (VB_DEV, 1), 0), flat_weight, 0.0)
    voxel_weight = lax.dot_general(
        hot_upper, hot_lower, (((1,), (1,)), ((), ())), precision=lax.Precision.HIGHEST
    ).reshape(-1)
    summed, weight_sum = (
        lax.psum_scatter(voxel_sum, ("orient", "frame"), scatter_dimension=0, tiled=True),
        lax.psum_scatter(voxel_weight, ("orient", "frame"), scatter_dimension=0, tiled=True),
    )
    return summed / (1.0 + weight_sum)[:, None]


def solution(mesh):
    placed = (
        P(("orient", "frame"), None),
        P(),
        P("orient", None),
        P("orient", None),
        P("orient", None),
    )
    return jax.shard_map(
        local, mesh=mesh, in_specs=placed, out_specs=P(("orient", "frame"), None), check_vma=False
    )
```

time: 1090 us -> 597 us (0.55)
  other arithmetic: 743 us -> 27.3 us
  waiting for transfers between devices: 107 us -> 284 us
  blocking collectives: 150 us -> 201 us
  Pallas kernels: 0 us -> 21.8 us
  local copies, waits for them, and re-layouts: 35.5 us -> 16.3 us
  matrix products: 43 us -> 31.3 us
    scatter-add x2 -> x0, other arithmetic: 725 us -> none  [the longest x1 383 us: local(): jax.ops.segment_sum(weighted.reshape(-1, 128), flat_target, num_segments=...]
    reduce_scatter x1, waiting for transfers between devices: 0.01 us -> 141 us  [local(): lax.psum_scatter(voxel_sum, ('orient', 'frame'), scatter_dimension=0, til...]
    reshape x1 -> x2, local copies, waits for them, and re-layouts: 35.5 us -> 5.4 us  [the longest x1 5.31 us: local(): (gathered + 0.25 * slice_part).reshape(orient_count, q_count, 128)]
    unnamed x1 -> x2, blocking collectives: 63.8 us -> 91.2 us
    reduce_scatter x0 -> x1, waiting for transfers between devices: none -> 24.5 us  [local(): scores = lax.psum_scatter(partial, 'frame', scatter_dimension=0, tiled=True)]
    pallas_call x0 -> x1, Pallas kernels: none -> 21.8 us  [scatter(): pl.pallas_call(functools.partial(scatter_kernel, q_count), out_shape=jax....]
    all_to_all x0 -> x1, blocking collectives: none -> 21.4 us  [local(): lax.all_to_all(own, 'frame', split_axis=1, concat_axis=0, tiled=True)]
    dot_general x2 -> x3, matrix products: 43 us -> 31.3 us  [the longest x1 15.2 us: local(): lax.dot_general(prob, frames, (((0,), (0,)), ((), ())), preferred_element...]
  transfers between devices with their start and end apart: 2 -> 4, of which waited for: 1 -> 4; matrix products, arithmetic and copies ran while one was open for 32% -> 2% of each run, Pallas kernels for 0% -> 0%
where the time goes in v1:
time: 597 us; the launch traced here: 596 us
  waiting for transfers between devices  284 us (48%)
  blocking collectives  201 us (34%)
  matrix products  31.3 us (5%)
  other arithmetic  27.3 us (5%)
  Pallas kernels  21.8 us (4%)
  local copies, waits for them, and re-layouts  16.3 us (3%)
  between operations  14 us (2%)
    reduce_scatter x1, waiting for transfers between devices, local(): lax.psum_scatter(voxel_sum, ('orient', 'frame'), scatter_dimension=0, til...  141 us
    all_gather x1, waiting for transfers between devices, local(): frames = lax.all_gather(column, 'orient', axis=0, tiled=True)  104 us
    unnamed x2, blocking collectives  91.2 us
    pmax x1, blocking collectives, local(): frame_peak = lax.pmax(jnp.max(scores, axis=1), 'orient')  40.3 us
    psum x1, blocking collectives, local(): frame_total = lax.psum(jnp.sum(shifted, axis=1), 'orient')  35.5 us
    reduce_scatter x1, waiting for transfers between devices, local(): scores = lax.psum_scatter(partial, 'frame', scatter_dimension=0, tiled=True)  24.5 us
    pallas_call x1, Pallas kernels, scatter(): pl.pallas_call(functools.partial(scatter_kernel, q_count), out_shape=jax....  21.8 us
    all_to_all x1, blocking collectives, local(): lax.all_to_all(own, 'frame', split_axis=1, concat_axis=0, tiled=True)  21.4 us
  transfers between devices with their start and end apart: 4, of which 4 were waited for; matrix products, arithmetic and copies ran while one was open for 2% of the time, Pallas kernels for 0%

profile of v1, /device:TPU:0, one launch (start us, length us, event | category | flops | bytes accessed | tf_op | source)
XLA Modules:
  0.0 596.5 jit_solution(12134888086811740199)
XLA Ops:
  6.5 1.8 multiply_convert_fusion
  8.3 0.1 copy.24
  8.4 21.4 %all_to_all.19 = bf16[32,8,2048]{2,0,1:T(8,128)(2,1)} all-to-all(bf16[32,8,2048]{2,0,1:T(8,128)(2,1)S(1)} %bitcast.20), channel_id=1, replica_groups=mesh['orient'=16,'frame'=8] {'frame'}, dimensions={1} | all-to-all | bytes 2097152 | tf_op jit(solution)/shard_map/all_to_all | solution.py:82
  29.8 0.0 all-gather.3.cloned.1.call-update
  29.8 0.0 reduce-scatter.3.cloned.1.call-start
  29.9 6.9 %convert_reduce_fusion = f32[512]{0:T(512)S(1)} fusion(bf16[512,16384]{1,0:T(8,128)(2,1)} %param.7), kind=kLoop, calls=%fused_computation | loop fusion | flops 16776704 | bytes 16779264 | tf_op jit(solution)/shard_map/reduce_sum | solution.py:84
  36.8 103.9 %all-gather.3.cloned.1.call-done = bf16[4096,2048]{1,0:T(8,128)(2,1)} async-done(((bf16[256,2048]{1,0:T(8,128)(2,1)}), bf16[4096,2048]{1,0:T(8,128)(2,1)}) %all-gather.3.cloned.1.call-update) | async-done | bytes 16777232 | tf_op jit(solution)/shard_map/all_gather | solution.py:83
  140.7 7.1 %convert_reduce_fusion.1 = f32[4096]{0:T(1024)S(1)} fusion(bf16[4096,2048]{1,0:T(8,128)(2,1)} %all-gather.3.cloned.1.call-done), kind=kLoop, calls=%fused_computation.1 | loop fusion | flops 16773120 | bytes 16793600 | tf_op jit(solution)/shard_map/reduce_sum | solution.py:87
  147.8 3.6 copy-done.1
  151.4 13.7 %subtract_multiply_fusion = f32[4096,512]{1,0:T(8,128)} fusion(bf16[4096,2048]{1,0:T(8,128)(2,1)S(1)} %copy-done.1, f32[512]{0:T(512)S(1)} %multiply_log_fusion, f32[4096]{0:T(1024)S(1)} %convert_reduce_fusion.1, bf16[512,16384]{1,0:T(8,128)(2,1)} %param.7, s32[]{:T(128)S(6)} %select_n.33), kind=kOutput, calls=%fused_computation.2 | convolution fusion | flops 8598323200 | bytes 27281412 | tf_op jit(solution)/shard_map/dot_general | solution.py:89
  165.1 0.0 reduce-scatter.3.cloned.1.call-update
  165.1 0.0 copy-start.2
  165.1 0.0 all-gather.5.cloned.1.call-start
  165.2 0.6 copy-done.3
  165.8 0.7 dynamic-slice
  167.1 26.2 %all-reduce = f32[4096]{0:T(1024)S(1)} all-reduce(f32[4096]{0:T(1024)S(1)} %convert_reduce_fusion.1), channel_id=3, replica_groups=mesh['orient'=16,'frame'=8] {'frame'}, use_global_device_ids=true, to_apply=%region_7.0.clone | all-reduce | flops 4096 | bytes 32768
  193.3 0.1 dynamic-slice_multiply_fusion
  193.4 24.5 %reduce-scatter.3.cloned.1.call-done = f32[512,512]{1,0:T(8,128)} async-done(((f32[4096,512]{1,0:T(8,128)}), f32[512,512]{1,0:T(8,128)}) %reduce-scatter.3.cloned.1.call-update) | async-done | bytes 1048592 | tf_op jit(solution)/shard_map/reduce_scatter | solution.py:93
  217.9 1.4 reduce_max.9
  219.3 40.3 %pmax.7 = f32[512]{0:T(512)S(1)} all-reduce(f32[512]{0:T(512)S(1)} %reduce_max.9), channel_id=1, replica_groups=mesh['orient'=16,'frame'=8] {'orient'}, use_global_device_ids=true, to_apply=%region_4.0 | all-reduce | flops 512 | bytes 4096 | tf_op jit(solution)/shard_map/pmax | solution.py:95
  259.6 1.5 fusion.8
  261.1 35.5 %psum.14 = f32[512]{0:T(512)S(1)} all-reduce(f32[512]{0:T(512)S(1)} %fusion.8), channel_id=1, replica_groups=mesh['orient'=16,'frame'=8] {'orient'}, use_global_device_ids=true, to_apply=%region_6.0 | all-reduce | flops 512 | bytes 4096 | tf_op jit(solution)/shard_map/psum | solution.py:97
  296.5 2.3 multiply_reduce_fusion
  298.9 0.0 all-gather.5.cloned.1.call-update
  298.9 0.0 reduce-scatter.5.cloned.1.call-start
  298.9 13.1 %psum.15 = f32[512]{0:T(512)S(1)} all-reduce(f32[512]{0:T(512)S(1)} %get-tuple-element.7), channel_id=1, replica_groups=mesh['orient'=16,'frame'=8] {'frame'}, use_global_device_ids=true, to_apply=%region_9.0 | all-reduce | flops 512 | bytes 4096 | tf_op jit(solution)/shard_map/psum | solution.py:99
  312.0 0.0 copy-done.2
  312.0 0.2 divide_bitcast_fusion
  312.2 0.1 copy.19
  312.3 14.6 %all-gather.5.cloned.1.call-done = bf16[4096,512]{1,0:T(8,128)(2,1)} async-done(((bf16[512,512]{1,0:T(8,128)(2,1)}), bf16[4096,512]{1,0:T(8,128)(2,1)}) %all-gather.5.cloned.1.call-update) | async-done | bytes 4194320 | tf_op jit(solution)/shard_map/all_gather | solution.py:100
  326.9 15.2 %fusion.1 = f32[512,2048]{1,0:T(8,128)} fusion(bf16[4096,512]{1,0:T(8,128)(2,1)} %all-gather.5.cloned.1.call-done, bf16[4096,2048]{1,0:T(8,128)(2,1)} %all-gather.3.cloned.1.call-done, bf16[512,16384]{1,0:T(8,128)(2,1)} %param.7, s32[]{:T(128)S(6)} %select_n.33), kind=kOutput, calls=%fused_computation.6 | convolution fusion | flops 8593080320 | bytes 27262980 | tf_op jit(solution)/shard_map/dot_general | solution.py:101
  342.2 5.3 copy.17
  347.5 5.3 copy.18
  352.8 4.2 bitcast_multiply_fusion.rows_ref
  357.1 21.8 %shard_map.55 = f32[6144,128]{1,0:T(8,128)} custom-call(s32[1]{0:T(128)} %bitcast.block_ref, f32[16,512,128]{2,1,0:T(8,128)} %bitcast_multiply_fusion.rows_ref, s32[512,128]{1,0:T(8,128)S(1)} %copy-done), custom_call_target="tpu_custom_call" | custom-call | tf_op jit(solution)/shard_map/pallas_call | solution.py:57
  378.9 0.0 reduce-scatter.5.cloned.1.call-update
  378.9 0.2 dynamic-slice_remainder_fusion
  379.1 0.1 rem.28
  379.2 0.1 div.51
  379.4 0.1 sign_compare_fusion
  379.5 0.1 ne.46
  379.7 0.1 broadcast_in_dim.17
  379.8 2.3 fusion.2
  382.2 0.1 reshape.77
  382.3 65.0 %all-reduce.1 = f32[6144]{0:T(1024)S(1)} all-reduce(f32[6144]{0:T(1024)S(1)} %reshape.77), channel_id=5, replica_groups=mesh['orient'=16,'frame'=8] {'orient','frame'}, use_global_device_ids=true, to_apply=%region_11.12.clone | all-reduce | flops 6144 | bytes 49152
  447.2 0.1 dynamic-slice_add_fusion
  447.3 141.2 %reduce-scatter.5.cloned.1.call-done = f32[48,128]{1,0:T(8,128)} async-done(((f32[6144,128]{1,0:T(8,128)}), f32[48,128]{1,0:T(8,128)}) %reduce-scatter.5.cloned.1.call-update) | async-done | bytes 24592 | tf_op jit(solution)/shard_map/reduce_scatter | solution.py:120
  588.5 1.4 broadcast_divide_fusion
  (8 shorter events, 0.0 us)
Async XLA Ops:
  6.5 134.2 %all-gather.3.cloned.1.call-start = ((), (), s32[]{:S(2)}) async-start(), calls=%async_computation.3 | async-start | bytes 17825792 | tf_op jit(solution)/shard_map/all_gather | solution.py:83
  29.8 188.1 %reduce-scatter.3.cloned.1.call-start = ((), (), s32[]{:S(2)}) async-start(), calls=%async_computation.4 | async-start | bytes 9437184 | tf_op jit(solution)/shard_map/reduce_scatter | solution.py:93
  140.7 10.7 %copy-start.1 = (bf16[4096,2048]{1,0:T(8,128)(2,1)S(1)}, bf16[4096,2048]{1,0:T(8,128)(2,1)}, u32[]{:S(2)}) copy-start(bf16[4096,2048]{1,0:T(8,128)(2,1)} %all-gather.3.cloned.1.call-done) | copy-start | bytes 50331652
  165.1 0.7 copy-start.3
  165.1 146.9 %copy-start.2 = (f32[512,128]{1,0:T(8,128)S(1)}, f32[512,128]{1,0:T(8,128)}, u32[]{:S(2)}) copy-start(f32[512,128]{1,0:T(8,128)} %param.9) | copy-start | bytes 786436
  165.1 161.8 %all-gather.5.cloned.1.call-start = ((), (), s32[]{:S(2)}) async-start(), calls=%async_computation.5 | async-start | bytes 4718592 | tf_op jit(solution)/shard_map/all_gather | solution.py:100
  298.9 289.7 %reduce-scatter.5.cloned.1.call-start = ((), (), s32[]{:S(2)}) async-start(), calls=%async_computation.6 | async-start | bytes 3170304 | tf_op jit(solution)/shard_map/reduce_scatter | solution.py:120
  352.8 4.2 copy-start
Sparse Core Ops, SparseCore 0:
  30.0 110.6 all-gather.2
  165.3 52.6 reduce-scatter.2
  299.0 27.8 all-gather.4
  379.0 209.4 reduce-scatter.4

commit v2 on v1

--- a/solution.py
+++ b/solution.py
@@ -11,6 +11,136 @@
 ACCS = 4
 
 score_beta = 1.5
+
+
+SIDE = 4
+ORDERS = ((0, 1, 2), (1, 2, 0), (2, 0, 1))
+
+
+def here():
+    orient, frame = lax.axis_index("orient"), lax.axis_index("frame")
+    return (orient // SIDE, orient % SIDE, frame // 2, frame % 2)
+
+
+def device(place):
+    x, y, z, core = place
+    return (x * SIDE + y, z * 2 + core)
+
+
+def moved(place, axis, step):
+    out = list(place)
+    out[axis] = (place[axis] + step) % SIDE
+    return tuple(out)
+
+
+def pick(ref, axis, value, ndim):
+    return ref.at[tuple(value if a == axis else slice(None) for a in range(ndim))]
+
+
+def sums_kernel(v_ref, w_ref, o_ref, pair_out, pair_in, s1, s1b, in1, s2, s2b, in2, s3, s3b, in3,
+                wsum, wpair_in, win1, w2, win2, w3, win3,
+                pair_sem, sem1, sem2, sem3, wpair_sem, wsem1, wsem2, wsem3):
+    me = here()
+    core = me[3]
+    sibling = (me[0], me[1], me[2], 1 - core)
+    barrier = pltpu.get_barrier_semaphore()
+    peers = [sibling] + [moved(me, a, d) for a in range(3) for d in (1, 2, 3)]
+    for peer in peers:
+        pl.semaphore_signal(barrier, inc=1, device_id=device(peer), device_id_type=pl.DeviceIdType.MESH)
+    for p in range(3):
+        pair_out[p] = v_ref[:, :, :, 1 - core, 16 * p:16 * p + 16, :].astype(jnp.bfloat16)
+    pl.semaphore_wait(barrier, len(peers))
+
+    def send(src, dst, sems, slot, place):
+        copy = pltpu.make_async_remote_copy(
+            src_ref=src, dst_ref=dst, send_sem=sems.at[0, slot], recv_sem=sems.at[1, slot],
+            device_id=device(place), device_id_type=pl.DeviceIdType.MESH)
+        copy.start()
+        return copy
+
+    pair = [send(pair_out.at[p], pair_in.at[p], pair_sem, p, sibling) for p in range(3)]
+    wpair = send(w_ref.at[1 - core], wpair_in, wpair_sem, 0, sibling)
+    first, second, third = [], [], []
+    for p in range(3):
+        axis = ORDERS[p][0]
+        pair[p].wait_recv()
+        total = v_ref[:, :, :, core, 16 * p:16 * p + 16, :] + pair_in[p].astype(jnp.float32)
+        s1[p] = total
+        s1b[p] = total.astype(jnp.bfloat16)
+        first.append([send(pick(s1b.at[p], axis, (me[axis] + d) % SIDE, 3), in1.at[p, d - 1], sem1, 3 * p + d - 1,
+                           moved(me, axis, d)) for d in (1, 2, 3)])
+    wpair.wait_recv()
+    wsum[...] = w_ref[core] + wpair_in[...]
+    wfirst = [send(wsum.at[(me[0] + d) % SIDE], win1.at[d - 1], wsem1, d - 1, moved(me, 0, d)) for d in (1, 2, 3)]
+    for p in range(3):
+        axis, nxt = ORDERS[p][0], ORDERS[p][1]
+        for copy in first[p]:
+            copy.wait_recv()
+        own = pick(s1.at[p], axis, me[axis], 3)[...]
+        total = own + in1[p, 0].astype(jnp.float32) + in1[p, 1].astype(jnp.float32) + in1[p, 2].astype(jnp.float32)
+        s2[p] = total
+        s2b[p] = total.astype(jnp.bfloat16)
+        dim = nxt - (1 if nxt > axis else 0)
+        second.append([send(pick(s2b.at[p], dim, (me[nxt] + d) % SIDE, 2), in2.at[p, d - 1], sem2, 3 * p + d - 1,
+                            moved(me, nxt, d)) for d in (1, 2, 3)])
+    for copy in wfirst:
+        copy.wait_recv()
+    w2[...] = wsum[me[0]] + win1[0] + win1[1] + win1[2]
+    wsecond = [send(w2, win2.at[d - 1], wsem2, d - 1, moved(me, 1, d)) for d in (1, 2, 3)]
+    for p in range(3):
+        axis, nxt, last = ORDERS[p]
+        for copy in second[p]:
+            copy.wait_recv()
+        dim = nxt - (1 if nxt > axis else 0)
+        own = pick(s2.at[p], dim, me[nxt], 2)[...]
+        total = own + in2[p, 0].astype(jnp.float32) + in2[p, 1].astype(jnp.float32) + in2[p, 2].astype(jnp.float32)
+        s3[p] = total
+        s3b[p] = total.astype(jnp.bfloat16)
+        third.append([send(s3b.at[p, (me[last] + d) % SIDE], in3.at[p, d - 1], sem3, 3 * p + d - 1,
+                           moved(me, last, d)) for d in (1, 2, 3)])
+    for copy in wsecond:
+        copy.wait_recv()
+    w3[...] = w2[...] + win2[0] + win2[1] + win2[2]
+    wthird = [send(w3, win3.at[d - 1], wsem3, d - 1, moved(me, 2, d)) for d in (1, 2, 3)]
+    for copy in wthird:
+        copy.wait_recv()
+    weights = w3[...] + win3[0] + win3[1] + win3[2]
+    mine = lax.broadcasted_iota(jnp.int32, weights.shape, 0) == me[1] * SIDE + me[2]
+    row = jnp.sum(jnp.where(mine, weights, 0.0), axis=0, keepdims=True)
+    shape = (o_ref.shape[0], 128)
+    diagonal = lax.broadcasted_iota(jnp.int32, shape, 0) == lax.broadcasted_iota(jnp.int32, shape, 1)
+    column = jnp.sum(jnp.where(diagonal, row, 0.0), axis=1, keepdims=True)
+    scale = 1.0 / (1.0 + column)
+    for p in range(3):
+        for copy in third[p]:
+            copy.wait_recv()
+        own = s3[p, me[ORDERS[p][2]]]
+        total = own + in3[p, 0].astype(jnp.float32) + in3[p, 1].astype(jnp.float32) + in3[p, 2].astype(jnp.float32)
+        o_ref[16 * p:16 * p + 16, :] = total * scale[16 * p:16 * p + 16]
+    for copies in pair, [wpair], *first, *second, *third, wfirst, wsecond, wthird:
+        for copy in copies:
+            copy.wait_send()
+
+
+def reduce_blocks(voxel_sum, voxel_weight):
+    f32, b16 = jnp.float32, jnp.bfloat16
+    vm, dma = pltpu.VMEM, pltpu.SemaphoreType.DMA
+    scratch = [
+        vm((3, 4, 4, 4, 16, 128), b16), vm((3, 4, 4, 4, 16, 128), b16),
+        vm((3, 4, 4, 4, 16, 128), f32), vm((3, 4, 4, 4, 16, 128), b16), vm((3, 3, 4, 4, 16, 128), b16),
+        vm((3, 4, 4, 16, 128), f32), vm((3, 4, 4, 16, 128), b16), vm((3, 3, 4, 16, 128), b16),
+        vm((3, 4, 16, 128), f32), vm((3, 4, 16, 128), b16), vm((3, 3, 16, 128), b16),
+        vm((4, 16, 128), f32), vm((4, 16, 128), f32), vm((3, 16, 128), f32),
+        vm((16, 128), f32), vm((3, 16, 128), f32), vm((16, 128), f32), vm((3, 16, 128), f32),
+        dma((2, 3)), dma((2, 9)), dma((2, 9)), dma((2, 9)), dma((2, 1)), dma((2, 3)), dma((2, 3)), dma((2, 3)),
+    ]
+    vspec = pl.BlockSpec(memory_space=pltpu.VMEM)
+    return pl.pallas_call(
+        sums_kernel,
+        out_shape=jax.ShapeDtypeStruct((48, 128), f32),
+        in_specs=[vspec, vspec], out_specs=vspec, scratch_shapes=scratch,
+        compiler_params=pltpu.CompilerParams(collective_id=3, has_side_effects=True, vmem_limit_bytes=40 * 2**20),
+    )(voxel_sum, voxel_weight)
 
 
 def scatter_kernel(q_count, block_ref, rows_ref, index_hbm, out_ref, index_smem, sem, *accs):
@@ -111,16 +241,16 @@
     targets = lax.dynamic_slice_in_dim(voxel_index, me * q_count, q_count, axis=1).reshape(1, -1)
     flat_weight = weight.reshape(1, -1)
     upper, lower = targets // VB_DEV, targets % VB_DEV
-    hot_upper = (upper == lax.broadcasted_iota(jnp.int32, (128, 1), 0)).astype(jnp.float32)
-    hot_lower = jnp.where(lower == lax.broadcasted_iota(jnp.int32, (VB_DEV, 1), 0), flat_weight, 0.0)
+    slot = lax.broadcasted_iota(jnp.int32, (128, 1), 0)
+    owner = 2 * (slot % 64) + slot // 64
+    hot_upper = (upper == owner).astype(jnp.float32)
+    hot_lower = jnp.where(lower == slot, flat_weight, 0.0)
     voxel_weight = lax.dot_general(
         hot_upper, hot_lower, (((1,), (1,)), ((), ())), precision=lax.Precision.HIGHEST
-    ).reshape(-1)
-    summed, weight_sum = (
-        lax.psum_scatter(voxel_sum, ("orient", "frame"), scatter_dimension=0, tiled=True),
-        lax.psum_scatter(voxel_weight, ("orient", "frame"), scatter_dimension=0, tiled=True),
-    )
-    return summed / (1.0 + weight_sum)[:, None]
+    )
+    return reduce_blocks(
+        voxel_sum.reshape(SIDE, SIDE, SIDE, 2, VB_DEV, 128), voxel_weight.reshape(2, SIDE, SIDE * SIDE, 128)
+    )
 
 
 def solution(mesh):

time: 597 us -> 405 us (0.68)
  waiting for transfers between devices: 284 us -> 139 us
  blocking collectives: 201 us -> 136 us
  Pallas kernels: 21.8 us -> 40.3 us
    reduce_scatter x1 -> x0, waiting for transfers between devices: 141 us -> none  [local(): lax.psum_scatter(voxel_sum, ('orient', 'frame'), scatter_dimension=0, til...]
    unnamed x2 -> x1, blocking collectives: 91.2 us -> 26.2 us
    pallas_call x0 -> x1, Pallas kernels: none -> 20.2 us  [reduce_blocks(): pl.pallas_call(sums_kernel, out_shape=jax.ShapeDtypeStruct((48, 128), f32...]
  transfers between devices with their start and end apart: 4 -> 3, of which waited for: 4 -> 3; matrix products, arithmetic and copies ran while one was open for 2% -> 3% of each run, Pallas kernels for 0% -> 0%
where the time goes in v2:
time: 405 us; the launch traced here: 404 us
  waiting for transfers between devices  139 us (34%)
  blocking collectives  136 us (34%)
  Pallas kernels  40.3 us (10%)
  matrix products  31.9 us (8%)
  other arithmetic  25.7 us (6%)
  local copies, waits for them, and re-layouts  16.8 us (4%)
  between operations  14 us (3%)
    all_gather x1, waiting for transfers between devices, local(): frames = lax.all_gather(column, 'orient', axis=0, tiled=True)  104 us
    pmax x1, blocking collectives, local(): frame_peak = lax.pmax(jnp.max(scores, axis=1), 'orient')  40.3 us
    psum x1, blocking collectives, local(): frame_total = lax.psum(jnp.sum(shifted, axis=1), 'orient')  35.5 us
    unnamed x1, blocking collectives  26.2 us
    reduce_scatter x1, waiting for transfers between devices, local(): scores = lax.psum_scatter(partial, 'frame', scatter_dimension=0, tiled=True)  24.5 us
    all_to_all x1, blocking collectives, local(): lax.all_to_all(own, 'frame', split_axis=1, concat_axis=0, tiled=True)  21.4 us
    pallas_call x1, Pallas kernels, reduce_blocks(): pl.pallas_call(sums_kernel, out_shape=jax.ShapeDtypeStruct((48, 128), f32...  20.2 us
    pallas_call x1, Pallas kernels, scatter(): pl.pallas_call(functools.partial(scatter_kernel, q_count), out_shape=jax....  20.1 us
  transfers between devices with their start and end apart: 3, of which 3 were waited for; matrix products, arithmetic and copies ran while one was open for 3% of the time, Pallas kernels for 0%

profile of v2, /device:TPU:0, one launch (start us, length us, event | category | flops | bytes accessed | tf_op | source)
XLA Modules:
  0.0 404.5 jit_solution(1846025895764984190)
XLA Ops:
  6.5 0.0 all-gather.3.cloned.1.call-start
  6.5 1.8 multiply_convert_fusion
  8.3 0.1 copy.20
  8.4 21.4 %all_to_all.19 = bf16[32,8,2048]{2,0,1:T(8,128)(2,1)} all-to-all(bf16[32,8,2048]{2,0,1:T(8,128)(2,1)S(1)} %bitcast.24), channel_id=1, replica_groups=mesh['orient'=16,'frame'=8] {'frame'}, dimensions={1} | all-to-all | bytes 2097152 | tf_op jit(solution)/shard_map/all_to_all | solution.py:212
  29.8 0.0 all-gather.3.cloned.1.call-update
  29.8 0.0 reduce-scatter.2.cloned.1.call-start
  29.9 6.9 %convert_reduce_fusion = f32[512]{0:T(512)S(1)} fusion(bf16[512,16384]{1,0:T(8,128)(2,1)} %param.7), kind=kLoop, calls=%fused_computation | loop fusion | flops 16776704 | bytes 16779264 | tf_op jit(solution)/shard_map/reduce_sum | solution.py:214
  36.8 103.9 %all-gather.3.cloned.1.call-done = bf16[4096,2048]{1,0:T(8,128)(2,1)} async-done(((bf16[256,2048]{1,0:T(8,128)(2,1)}), bf16[4096,2048]{1,0:T(8,128)(2,1)}) %all-gather.3.cloned.1.call-update) | async-done | bytes 16777232 | tf_op jit(solution)/shard_map/all_gather | solution.py:213
  140.7 0.0 copy-start.1
  140.7 7.1 %convert_reduce_fusion.1 = f32[4096]{0:T(1024)S(1)} fusion(bf16[4096,2048]{1,0:T(8,128)(2,1)} %all-gather.3.cloned.1.call-done), kind=kLoop, calls=%fused_computation.1 | loop fusion | flops 16773120 | bytes 16793600 | tf_op jit(solution)/shard_map/reduce_sum | solution.py:217
  147.8 3.6 copy-done.1
  151.4 13.7 %subtract_multiply_fusion = f32[4096,512]{1,0:T(8,128)} fusion(bf16[4096,2048]{1,0:T(8,128)(2,1)S(1)} %copy-done.1, f32[512]{0:T(512)S(1)} %multiply_log_fusion, f32[4096]{0:T(1024)S(1)} %convert_reduce_fusion.1, bf16[512,16384]{1,0:T(8,128)(2,1)} %param.7, s32[]{:T(128)S(6)} %select_n.54), kind=kOutput, calls=%fused_computation.2 | convolution fusion | flops 8598323200 | bytes 27281412 | tf_op jit(solution)/shard_map/dot_general | solution.py:219
  165.1 0.0 copy-start.3
  165.1 0.0 reduce-scatter.2.cloned.1.call-update
  165.1 0.0 copy-start
  165.1 0.0 copy-start.2
  165.2 0.0 all-gather.5.cloned.1.call-start
  165.2 0.6 copy-done.3
  165.8 0.7 dynamic-slice
  167.1 26.2 %all-reduce = f32[4096]{0:T(1024)S(1)} all-reduce(f32[4096]{0:T(1024)S(1)} %convert_reduce_fusion.1), channel_id=3, replica_groups=mesh['orient'=16,'frame'=8] {'frame'}, use_global_device_ids=true, to_apply=%region_7.0.clone | all-reduce | flops 4096 | bytes 32768
  193.3 0.1 dynamic-slice_multiply_fusion
  193.4 24.5 %reduce-scatter.2.cloned.1.call-done = f32[512,512]{1,0:T(8,128)} async-done(((f32[4096,512]{1,0:T(8,128)}), f32[512,512]{1,0:T(8,128)}) %reduce-scatter.2.cloned.1.call-update) | async-done | bytes 1048592 | tf_op jit(solution)/shard_map/reduce_scatter | solution.py:223
  217.9 1.4 reduce_max.9
  219.3 40.3 %pmax.7 = f32[512]{0:T(512)S(1)} all-reduce(f32[512]{0:T(512)S(1)} %reduce_max.9), channel_id=1, replica_groups=mesh['orient'=16,'frame'=8] {'orient'}, use_global_device_ids=true, to_apply=%region_4.0 | all-reduce | flops 512 | bytes 4096 | tf_op jit(solution)/shard_map/pmax | solution.py:225
  259.6 1.5 fusion.13
  261.1 35.5 %psum.14 = f32[512]{0:T(512)S(1)} all-reduce(f32[512]{0:T(512)S(1)} %fusion.13), channel_id=1, replica_groups=mesh['orient'=16,'frame'=8] {'orient'}, use_global_device_ids=true, to_apply=%region_6.0 | all-reduce | flops 512 | bytes 4096 | tf_op jit(solution)/shard_map/psum | solution.py:227
  296.5 2.3 multiply_reduce_fusion
  298.9 0.0 all-gather.5.cloned.1.call-update
  298.9 0.0 copy-done
  298.9 0.2 dynamic-slice_divide_fusion
  299.1 0.1 div.51
  299.2 0.1 sign_compare_fusion
  299.4 0.1 ne.86
  299.5 0.1 rem.44
  299.7 13.1 %psum.15 = f32[512]{0:T(512)S(1)} all-reduce(f32[512]{0:T(512)S(1)} %get-tuple-element.7), channel_id=1, replica_groups=mesh['orient'=16,'frame'=8] {'frame'}, use_global_device_ids=true, to_apply=%region_9.0 | all-reduce | flops 512 | bytes 4096 | tf_op jit(solution)/shard_map/psum | solution.py:229
  312.8 0.0 copy-done.2
  312.8 0.2 divide_bitcast_fusion
  313.0 0.1 copy.17
  313.1 0.1 broadcast_in_dim.26
  313.3 2.9 fusion.2
  316.2 10.8 %all-gather.5.cloned.1.call-done = bf16[4096,512]{1,0:T(8,128)(2,1)} async-done(((bf16[512,512]{1,0:T(8,128)(2,1)}), bf16[4096,512]{1,0:T(8,128)(2,1)}) %all-gather.5.cloned.1.call-update) | async-done | bytes 4194320 | tf_op jit(solution)/shard_map/all_gather | solution.py:230
  326.9 15.2 %fusion.1 = f32[512,2048]{1,0:T(8,128)} fusion(bf16[4096,512]{1,0:T(8,128)(2,1)} %all-gather.5.cloned.1.call-done, bf16[4096,2048]{1,0:T(8,128)(2,1)} %all-gather.3.cloned.1.call-done, bf16[512,16384]{1,0:T(8,128)(2,1)} %param.7, s32[]{:T(128)S(6)} %select_n.54), kind=kOutput, calls=%fused_computation.6 | convolution fusion | flops 8593080320 | bytes 27262980 | tf_op jit(solution)/shard_map/dot_general | solution.py:231
  342.2 5.3 %copy.15 = f32[512,2048]{0,1:T(8,128)} copy(f32[512,2048]{1,0:T(8,128)} %fusion.1) | data formatting | bytes 8388608 | tf_op jit(solution)/shard_map/add | solution.py:237
  347.5 5.3 %copy.16 = f32[512,16,128]{2,0,1:T(8,128)} copy(f32[512,16,128]{0,2,1:T(8,128)} %bitcast.21) | data formatting | bytes 8388608 | tf_op jit(solution)/shard_map/reshape | solution.py:237
  352.8 4.2 %bitcast_multiply_fusion.rows_ref = f32[16,512,128]{2,1,0:T(8,128)} fusion(f32[512,16,128]{2,0,1:T(8,128)} %copy.16, f32[16,512]{1,0:T(8,128)S(1)} %copy.17), kind=kLoop, calls=%fused_computation.7 | loop fusion | flops 1048576 | bytes 8421376 | tf_op jit(solution)/shard_map/mul | solution.py:238
  357.0 20.1 %shard_map.55 = f32[6144,128]{1,0:T(8,128)S(1)} custom-call(s32[1]{0:T(128)} %bitcast.block_ref, f32[16,512,128]{2,1,0:T(8,128)} %bitcast_multiply_fusion.rows_ref, s32[512,128]{1,0:T(8,128)S(1)} %copy-done), custom_call_target="tpu_custom_call" | custom-call | tf_op jit(solution)/shard_map/pallas_call | solution.py:187
  377.1 20.2 %shard_map.56 = f32[48,128]{1,0:T(8,128)S(1)} custom-call(f32[4,4,4,2,48,128]{5,4,3,2,1,0:T(8,128)S(1)} %bitcast.19, f32[2,4,16,128]{3,2,1,0:T(8,128)S(1)} %bitcast.20), custom_call_target="tpu_custom_call" | custom-call | tf_op jit(solution)/shard_map/pallas_call | solution.py:138
  397.3 0.6 copy.22
  (4 shorter events, 0.0 us)
Async XLA Ops:
  6.5 134.2 %all-gather.3.cloned.1.call-start = ((), (), s32[]{:S(2)}) async-start(), calls=%async_computation.2 | async-start | bytes 17825792 | tf_op jit(solution)/shard_map/all_gather | solution.py:213
  29.8 188.1 %reduce-scatter.2.cloned.1.call-start = ((), (), s32[]{:S(2)}) async-start(), calls=%async_computation.3 | async-start | bytes 9437184 | tf_op jit(solution)/shard_map/reduce_scatter | solution.py:223
  140.7 10.7 %copy-start.1 = (bf16[4096,2048]{1,0:T(8,128)(2,1)S(1)}, bf16[4096,2048]{1,0:T(8,128)(2,1)}, u32[]{:S(2)}) copy-start(bf16[4096,2048]{1,0:T(8,128)(2,1)} %all-gather.3.cloned.1.call-done) | copy-start | bytes 50331652
  165.1 0.7 copy-start.3
  165.1 133.8 %copy-start = (s32[512,128]{1,0:T(8,128)S(1)}, s32[512,128]{1,0:T(8,128)}, u32[]{:S(2)}) copy-start(s32[512,128]{1,0:T(8,128)} %index_hbm.1) | copy-start | bytes 786436
  165.1 147.7 %copy-start.2 = (f32[512,128]{1,0:T(8,128)S(1)}, f32[512,128]{1,0:T(8,128)}, u32[]{:S(2)}) copy-start(f32[512,128]{1,0:T(8,128)} %param.9) | copy-start | bytes 786436
  165.2 161.8 %all-gather.5.cloned.1.call-start = ((), (), s32[]{:S(2)}) async-start(), calls=%async_computation.4 | async-start | bytes 4718592 | tf_op jit(solution)/shard_map/all_gather | solution.py:230
Sparse Core Ops, SparseCore 0:
  30.0 110.6 all-gather.2
  165.3 52.6 reduce-scatter.1
  299.0 27.8 all-gather.4

commit v3 on v2

--- a/solution.py
+++ b/solution.py
@@ -9,8 +9,6 @@
 
 VB_DEV = 48
 ACCS = 4
-
-score_beta = 1.5
 
 
 SIDE = 4
@@ -143,6 +141,375 @@
     )(voxel_sum, voxel_weight)
 
 
+PARTS = 8
+PART = 2048
+HALF = 256
+HELD = 272
+score_beta = 1.5
+NT = (((1,), (1,)), ((), ()))
+
+
+def iterate_kernel(counts_ref, gain_ref, interp_ref, slices_hbm, rows_ref,
+                   own, frames, part, stream, logs, log_mean, scores, pair_in, blocks, z1_in, kept, z2_in,
+                   shifted, photon, stat, stat2, stat3, sib_in, x_in, y_in, prob, gathered, mass,
+                   load_sem, a2a_send, a2a_recv, g_send, g_recv, pair_sem, z1_sem, z2_sem, sib_sem,
+                   x_send, x_recv, y_send, y_recv, ag1_sem, ag2_sem, agc_sem):
+    f32, b16 = jnp.float32, jnp.bfloat16
+    x, y, z, core = me = here()
+    plane = z * 2 + core
+    pixel_count = PARTS * PART
+    sibling = (x, y, z, 1 - core)
+    near = (x, y, z + 1 - 2 * (z % 2), core)
+    far = (x, y, 3 - z, core)
+    group = ((z + 1) // 2) % 2
+    spot = z // 2
+    xl, xr, yl, yr = (x + 3) % 4, (x + 1) % 4, (y + 3) % 4, (y + 1) % 4
+    to_xr, to_xl = (xr, y, z, core), (xl, y, z, core)
+    to_yr, to_yl = (x, yr, z, core), (x, yl, z, core)
+
+    def remote(src, dst, send_sem, recv_sem, place):
+        return pltpu.make_async_remote_copy(
+            src_ref=src, dst_ref=dst, send_sem=send_sem, recv_sem=recv_sem,
+            device_id=device(place), device_id_type=pl.DeviceIdType.MESH)
+
+    def when(s, body, limit=PARTS):
+        pl.when((s >= 0) & (s < limit))(lambda: body(s))
+
+    load = pltpu.make_async_copy(
+        slices_hbm.at[:, pl.ds(pl.multiple_of(plane * PART, PART), PART)], part, load_sem.at[0])
+    load.start()
+
+    def stream_copy(j):
+        return pltpu.make_async_copy(
+            slices_hbm.at[pl.ds(pl.multiple_of(core * HALF, HALF), HALF), pl.ds(pl.multiple_of(j * PART, PART), PART)],
+            stream.at[j % 2], load_sem.at[1 + j % 2])
+
+    stream_copy(0).start()
+    stream_copy(1).start()
+
+    barrier = pltpu.get_barrier_semaphore()
+    column = [(plane + d) % PARTS for d in range(1, PARTS)]
+    peers = [(x, y, k // 2, k % 2) for k in column]
+    peers += [moved(me, 0, d) for d in (1, 2, 3)] + [moved(me, 1, d) for d in (1, 2, 3)]
+    for peer in peers:
+        pl.semaphore_signal(barrier, inc=1, device_id=device(peer), device_id_type=pl.DeviceIdType.MESH)
+
+    def correct(j, carry):
+        lanes = pl.ds(pl.multiple_of(j * PART, PART), PART)
+        own[j] = (counts_ref[:, lanes].astype(f32) * gain_ref[:, lanes]).astype(b16)
+        return carry
+
+    lax.fori_loop(0, PARTS, correct, 0)
+    frames[plane, x, y] = own[plane]
+    pl.semaphore_wait(barrier, len(peers))
+
+    def a2a_copy(d):
+        k = (plane + d) % PARTS
+        return remote(own.at[k], frames.at[plane, x, y], a2a_send.at[d - 1], a2a_recv.at[plane], (x, y, k // 2, k % 2))
+
+    def a2a_start(d, carry):
+        a2a_copy(d).start()
+        return carry
+
+    lax.fori_loop(1, PARTS, a2a_start, 0)
+
+    def order(i):
+        return jnp.where(i == 0, plane, jnp.where(i - 1 < plane, i - 1, i))
+
+    def gather_copy(i, n):
+        s = order(i)
+        lo, hi = pl.ds(0, 16), pl.ds(16, 16)
+        left, right = pl.ds(0, PART // 2), pl.ds(PART // 2, PART // 2)
+        two, other = pl.ds(0, 2), pl.ds(2, 2)
+        every = pl.ds(0, 4)
+        full = pl.ds(0, PART)
+        where, place = [
+            ((s, x, y, lo, full), to_xr), ((s, x, y, lo, full), to_xl),
+            ((s, x, y, hi, full), to_yr), ((s, x, y, hi, full), to_yl),
+            ((s, xl, y, lo, left), to_xr), ((s, xr, y, lo, right), to_xl),
+            ((s, x, yl, hi, left), to_yr), ((s, x, yr, hi, right), to_yl),
+            ((s, every, y, lo, full), to_yr), ((s, every, y, lo, full), to_yl),
+            ((s, x, every, hi, full), to_xr), ((s, x, every, hi, full), to_xl),
+            ((s, two, yl, lo, full), to_yr), ((s, other, yr, lo, full), to_yl),
+            ((s, xl, two, hi, full), to_xr), ((s, xr, other, hi, full), to_xl),
+        ][n]
+        return remote(frames.at[where], frames.at[where], g_send.at[i, n], g_recv.at[i, n], place)
+
+    def gather(stage):
+        def body(i):
+            if stage == 1:
+                s = order(i)
+
+                @pl.when(s != plane)
+                def _():
+                    remote(own.at[0], frames.at[s, x, y], a2a_send.at[0], a2a_recv.at[s], sibling).wait_recv()
+            else:
+                for n in range(4 * stage - 8, 4 * stage - 4):
+                    gather_copy(i, n).wait_recv()
+            if stage < 5:
+                for n in range(4 * stage - 4, 4 * stage):
+                    gather_copy(i, n).start()
+        return body
+
+    when(0, gather(1))
+
+    log_mean[...] = jnp.zeros_like(log_mean)
+
+    def add_means(j, carry):
+        stream_copy(j).wait()
+        log_mean[...] += jnp.dot(stream[j % 2], jnp.ones((PART, 128), b16), preferred_element_type=f32)
+
+        @pl.when(j + 2 < PARTS)
+        def _():
+            stream_copy(j + 2).start()
+        return carry
+
+    lax.fori_loop(0, PARTS, add_means, 0)
+    log_mean[...] = jnp.log(log_mean[...] / pixel_count)
+    gather(2)(0)
+    load.wait()
+
+    def take_logs(h):
+        def body(j, carry):
+            rows = pl.ds(pl.multiple_of(j * 16, 16), 16)
+            logs[h, rows, :] = jnp.log(part[pl.ds(pl.multiple_of(h * HALF + j * 16, 16), 16), :].astype(f32)).astype(b16)
+            return carry
+        lax.fori_loop(0, HALF // 16, body, 0)
+        logs[h, HALF:HELD, :] = jnp.ones((HELD - HALF, PART), b16)
+
+    take_logs(0)
+    gather(3)(0)
+    gather(1)(1)
+    take_logs(1)
+    gather(2)(1)
+    gather(1)(2)
+    weight = interp_ref[...]
+    weight_hi = weight.astype(b16)
+    weight_lo = (weight - weight_hi.astype(f32)).astype(b16)
+
+    def spread(j, carry):
+        lane = lax.broadcasted_iota(jnp.int32, (128, 256), 0)
+        column_of = plane * 16 + 2 * j + lax.broadcasted_iota(jnp.int32, (128, 256), 1) // 128
+        hot = jnp.where(lane == column_of, 1.0, 0.0).astype(b16)
+        out = jnp.dot(weight_hi, hot, preferred_element_type=f32) + jnp.dot(weight_lo, hot, preferred_element_type=f32)
+        rows_ref[2 * j] = out[:, :128]
+        rows_ref[2 * j + 1] = out[:, 128:]
+        return carry
+
+    lax.fori_loop(0, PARTS, spread, 0)
+    mass[...] = jnp.zeros_like(mass)
+
+    def clear(j, carry):
+        gathered[pl.ds(pl.multiple_of(j * 16, 16), 16), :] = jnp.zeros((16, PART), f32)
+        return carry
+
+    lax.fori_loop(0, 2 * HALF // 16, clear, 0)
+
+    def pair_copy(s):
+        return remote(scores.at[s % 2, 1 - core], pair_in.at[s], pair_sem.at[0, s], pair_sem.at[1, s], sibling)
+
+    def z1_copy(s):
+        return remote(blocks.at[s % 2, 1 - group], z1_in.at[s], z1_sem.at[0, s], z1_sem.at[1, s], near)
+
+    def z2_copy(s):
+        return remote(kept.at[s % 2, 1 - spot], z2_in.at[s], z2_sem.at[0, s], z2_sem.at[1, s], far)
+
+    def sib_copy(s):
+        return remote(stat.at[s % 2], sib_in.at[s], sib_sem.at[0, s], sib_sem.at[1, s], sibling)
+
+    def x_copy(s, d):
+        return remote(stat2.at[s % 2], x_in.at[s, d - 1], x_send.at[s, d - 1], x_recv.at[s, d - 1], moved(me, 0, d))
+
+    def y_copy(s, d):
+        return remote(stat3.at[s % 2], y_in.at[s, d - 1], y_send.at[s, d - 1], y_recv.at[s, d - 1], moved(me, 1, d))
+
+    def ag1_copy(s):
+        lanes = pl.ds(pl.multiple_of(z * 128, 128), 128)
+        return remote(prob.at[s, core, :, lanes], prob.at[s, core, :, lanes], ag1_sem.at[0, s], ag1_sem.at[1, s], near)
+
+    def ag2_copy(s):
+        lanes = pl.ds(pl.multiple_of(spot * 256, 256), 256)
+        return remote(prob.at[s, core, :, lanes], prob.at[s, core, :, lanes], ag2_sem.at[0, s], ag2_sem.at[1, s], far)
+
+    def agc_copy(s):
+        return remote(prob.at[s, core], prob.at[s, core], agc_sem.at[0, s], agc_sem.at[1, s], sibling)
+
+    def multiply(s):
+        pl.when(s >= 2)(lambda: pair_copy(s - 2).wait_send())
+
+        def tile(j, carry):
+            block = frames[s, pl.ds(2 * j, 2)].reshape(HALF, PART)
+            lanes = pl.ds(pl.multiple_of(j * HALF, HALF), HALF)
+            for h in range(2):
+                scores[s % 2, h, :, lanes] = lax.dot_general(logs[h], block, NT, preferred_element_type=f32)
+            return carry
+
+        lax.fori_loop(0, 2, tile, 0)
+        pair_copy(s).start()
+
+    def add_pair(s):
+        pl.when(s >= 2)(lambda: z1_copy(s - 2).wait_send())
+        pair_copy(s).wait_recv()
+        for b, (g, n) in enumerate(((0, 0), (1, 0), (1, 1), (0, 1))):
+            lanes = slice(128 * b, 128 * b + 128)
+            blocks[s % 2, g, n] = scores[s % 2, core, :, lanes] + pair_in[s, :, lanes]
+        z1_copy(s).start()
+
+    def add_near(s):
+        pl.when(s >= 2)(lambda: z2_copy(s - 2).wait_send())
+        z1_copy(s).wait_recv()
+        kept[s % 2] = blocks[s % 2, group] + z1_in[s]
+        z2_copy(s).start()
+
+    first_row = lax.broadcasted_iota(jnp.int32, (8, 128), 0) == 0
+
+    def combine(tiles):
+        peak = tiles[0][0:1]
+        for tile in tiles[1:]:
+            peak = jnp.maximum(peak, tile[0:1])
+        total = sum(tile[1:2] * jnp.exp(tile[0:1] - peak) for tile in tiles)
+        return peak, total
+
+    def score(s):
+        pl.when(s >= 2)(lambda: sib_copy(s - 2).wait_send())
+        z2_copy(s).wait_recv()
+        total = kept[s % 2, spot] + z2_in[s]
+        photons = total[HALF:HALF + 1]
+        value = (total[:HALF] - photons * log_mean[...]) * (score_beta / pixel_count)
+        peak = jnp.max(value, axis=0, keepdims=True)
+        value = jnp.exp(value - peak)
+        shifted[s % 2] = value
+        photon[s % 2] = jnp.broadcast_to(photons, (8, 128))
+        stat[s % 2] = jnp.where(first_row, peak, jnp.sum(value, axis=0, keepdims=True))
+        sib_copy(s).start()
+
+    def add_sibling(s):
+        pl.when(s >= 2)(lambda: [x_copy(s - 2, d).wait_send() for d in (1, 2, 3)] and None)
+        sib_copy(s).wait_recv()
+        peak, total = combine([stat[s % 2], sib_in[s]])
+        stat2[s % 2] = jnp.where(first_row, peak, total)
+        for d in (1, 2, 3):
+            x_copy(s, d).start()
+
+    def add_x(s):
+        pl.when(s >= 2)(lambda: [y_copy(s - 2, d).wait_send() for d in (1, 2, 3)] and None)
+        for d in (1, 2, 3):
+            x_copy(s, d).wait_recv()
+        peak, total = combine([stat2[s % 2], x_in[s, 0], x_in[s, 1], x_in[s, 2]])
+        stat3[s % 2] = jnp.where(first_row, peak, total)
+        for d in (1, 2, 3):
+            y_copy(s, d).start()
+
+    def normalise(s):
+        for d in (1, 2, 3):
+            y_copy(s, d).wait_recv()
+        peak, total = combine([stat3[s % 2], y_in[s, 0], y_in[s, 1], y_in[s, 2]])
+        factor = jnp.exp(stat[s % 2][0:1] - peak) / total
+        lanes = pl.ds(pl.multiple_of(z * 128, 128), 128)
+        prob[s, core, :HALF, lanes] = (shifted[s % 2] * factor).astype(b16)
+        photons = photon[s % 2][0:1]
+        upper = photons.astype(b16).astype(f32)
+        row = lax.broadcasted_iota(jnp.int32, (HELD - HALF, 128), 0)
+        prob[s, core, HALF:, lanes] = jnp.where(row == 0, upper, jnp.where(row == 1, photons - upper, 0.0)).astype(b16)
+        ag1_copy(s).start()
+
+    def spread_near(s):
+        ag1_copy(s).wait_recv()
+        ag2_copy(s).start()
+
+    def spread_far(s):
+        ag2_copy(s).wait_recv()
+        agc_copy(s).start()
+
+    def gather_pixels(s):
+        agc_copy(s).wait_recv()
+        for h in range(2):
+            mass[h] += lax.dot_general(prob[s, h, :HALF], prob[s, 0, HALF:], NT, preferred_element_type=f32)
+
+        def tile(j, carry):
+            lanes = pl.ds(pl.multiple_of(j * 256, 256), 256)
+            block = frames[s, :, :, :, lanes].reshape(2 * HALF, 256)
+            for h in range(2):
+                gathered[h * HALF:h * HALF + HALF, lanes] += jnp.dot(prob[s, h, :HALF], block, preferred_element_type=f32)
+            return carry
+
+        lax.fori_loop(0, PARTS, tile, 0)
+
+    def tick(t, carry):
+        when(t + 2, gather(3))
+        when(t + 3, gather(2))
+        when(t + 4, gather(1))
+        when(t + 1, gather(4))
+        when(t, gather(5))
+        when(t - 1, multiply)
+        when(t - 2, score)
+        when(t - 3, spread_near)
+        when(t - 1, add_pair)
+        when(t - 2, add_sibling)
+        when(t - 3, spread_far)
+        when(t - 2, add_x)
+        when(t - 1, add_near)
+        when(t - 2, normalise)
+        when(t - 3, gather_pixels)
+        return carry
+
+    lax.fori_loop(-1, PARTS + 3, tick, 0)
+
+    share = 1.0 / (jnp.sum(mass[...], axis=2, keepdims=True) * (1.0 / pixel_count) + 0.25)
+    for q in range(PART // 128):
+        for h in range(2):
+            lanes, some = slice(128 * q, 128 * q + 128), slice(h * HALF, h * HALF + HALF)
+            rows_ref[q, some] = rows_ref[q, some] * (
+                (gathered[some, lanes] + 0.25 * part[some, lanes].astype(f32)) * share[h])
+
+    def drain(i, carry):
+        for n in range(16):
+            gather_copy(i, n).wait_send()
+        ag1_copy(i).wait_send()
+        ag2_copy(i).wait_send()
+        agc_copy(i).wait_send()
+        return carry
+
+    lax.fori_loop(0, PARTS, drain, 0)
+
+    def drain_a2a(d, carry):
+        a2a_copy(d).wait_send()
+        return carry
+
+    lax.fori_loop(1, PARTS, drain_a2a, 0)
+    for s in (PARTS - 2, PARTS - 1):
+        pair_copy(s).wait_send()
+        z1_copy(s).wait_send()
+        z2_copy(s).wait_send()
+        sib_copy(s).wait_send()
+        for d in (1, 2, 3):
+            x_copy(s, d).wait_send()
+            y_copy(s, d).wait_send()
+
+
+def iterate(counts, gain, interp, slices):
+    f32, b16 = jnp.float32, jnp.bfloat16
+    vm, dma = pltpu.VMEM, pltpu.SemaphoreType.DMA
+    n = PARTS
+    scratch = [
+        vm((n, 32, PART), b16), vm((n, 4, 4, 32, PART), b16), vm((2 * HALF, PART), b16), vm((2, HALF, PART), b16),
+        vm((2, HELD, PART), b16), vm((HALF, 128), f32), vm((2, 2, HELD, 512), f32), vm((n, HELD, 512), f32),
+        vm((2, 2, 2, HELD, 128), f32), vm((n, 2, HELD, 128), f32), vm((2, 2, HELD, 128), f32), vm((n, HELD, 128), f32),
+        vm((2, HALF, 128), f32), vm((2, 8, 128), f32), vm((2, 8, 128), f32), vm((2, 8, 128), f32), vm((2, 8, 128), f32),
+        vm((n, 8, 128), f32), vm((n, 3, 8, 128), f32), vm((n, 3, 8, 128), f32),
+        vm((n, 2, HELD, 512), b16), vm((2 * HALF, PART), f32), vm((2, HALF, HELD - HALF), f32),
+        dma((3,)), dma((n - 1,)), dma((n,)), dma((n, 16)), dma((n, 16)), dma((2, n)), dma((2, n)), dma((2, n)), dma((2, n)),
+        dma((n, 3)), dma((n, 3)), dma((n, 3)), dma((n, 3)), dma((2, n)), dma((2, n)), dma((2, n)),
+    ]
+    vspec, anyspec = pl.BlockSpec(memory_space=pltpu.VMEM), pl.BlockSpec(memory_space=pl.ANY)
+    return pl.pallas_call(
+        iterate_kernel,
+        out_shape=jax.ShapeDtypeStruct((PART // 128, 2 * HALF, 128), f32),
+        in_specs=[vspec, vspec, vspec, anyspec], out_specs=vspec, scratch_shapes=scratch,
+        compiler_params=pltpu.CompilerParams(collective_id=2, has_side_effects=True, vmem_limit_bytes=62 * 2**20),
+    )(counts, gain.reshape(1, -1), interp, slices)
+
+
 def scatter_kernel(q_count, block_ref, rows_ref, index_hbm, out_ref, index_smem, sem, *accs):
     copy = pltpu.make_async_copy(index_hbm, index_smem, sem)
     copy.start()
@@ -203,41 +570,12 @@
     frame_size = lax.axis_size("frame")
     orient_size = lax.axis_size("orient")
     me = lax.axis_index("frame")
-    pixel_count = slices.shape[1]
-    orient_count = slices.shape[0]
-    part = pixel_count // frame_size
-    q_count = part // 128
+    q_count = PART // 128
     voxels = VB_DEV * orient_size * frame_size
-    own = (counts.astype(jnp.float32) * pixel_gain[None, :]).astype(jnp.bfloat16)
-    column = lax.all_to_all(own, "frame", split_axis=1, concat_axis=0, tiled=True)
-    frames = lax.all_gather(column, "orient", axis=0, tiled=True)
-    log_mean = jnp.log(jnp.sum(slices, axis=1, dtype=jnp.float32) / pixel_count)
-    slice_part = lax.dynamic_slice_in_dim(slices, me * part, part, axis=1).astype(jnp.float32)
-    log_slices = jnp.log(slice_part).astype(jnp.bfloat16)
-    photons_part = jnp.sum(frames, axis=1, dtype=jnp.float32)
-    score_scale = score_beta / pixel_count
-    products = lax.dot_general(
-        frames, log_slices, (((1,), (1,)), ((), ())), preferred_element_type=jnp.float32
-    )
-    partial = (products - photons_part[:, None] * log_mean[None, :]) * score_scale
-    scores = lax.psum_scatter(partial, "frame", scatter_dimension=0, tiled=True)
-    photons = lax.psum_scatter(photons_part, "frame", scatter_dimension=0, tiled=True)
-    frame_peak = lax.pmax(jnp.max(scores, axis=1), "orient")
-    shifted = jnp.exp(scores - frame_peak[:, None])
-    frame_total = lax.psum(jnp.sum(shifted, axis=1), "orient")
-    probability = shifted / frame_total[:, None]
-    mass = lax.psum(jnp.sum(probability * (photons / pixel_count)[:, None], axis=0), "frame")
-    prob = lax.all_gather(probability.astype(jnp.bfloat16), "frame", axis=0, tiled=True)
-    gathered = lax.dot_general(
-        prob, frames, (((0,), (0,)), ((), ())), preferred_element_type=jnp.float32
-    )
-    index = voxel_index
+    rows = iterate(counts, pixel_gain, interp, slices)
+    block = jnp.full((1,), me, jnp.int32)
+    voxel_sum = scatter(rows, voxel_index, block, voxels)
     weight = lax.dynamic_slice_in_dim(interp, me * q_count, q_count, axis=1)
-    share = weight / (mass + 0.25)[:, None]
-    rows = (gathered + 0.25 * slice_part).reshape(orient_count, q_count, 128).transpose(1, 0, 2)
-    rows = rows * share.T[:, :, None]
-    block = jnp.full((1,), me, jnp.int32)
-    voxel_sum = scatter(rows, index, block, voxels)
     targets = lax.dynamic_slice_in_dim(voxel_index, me * q_count, q_count, axis=1).reshape(1, -1)
     flat_weight = weight.reshape(1, -1)
     upper, lower = targets // VB_DEV, targets % VB_DEV

time: 405 us -> 249 us (0.61)
  Pallas kernels: 40.3 us -> 239 us
  waiting for transfers between devices: 139 us -> 0 us
  blocking collectives: 136 us -> 0 us
  matrix products: 31.9 us -> 2.89 us
  other arithmetic: 25.7 us -> 1.14 us
  between operations: 14 us -> 0.1 us
  local copies, waits for them, and re-layouts: 16.8 us -> 5.76 us
    pallas_call x0 -> x1, Pallas kernels: none -> 200 us  [iterate(): pl.pallas_call(iterate_kernel, out_shape=jax.ShapeDtypeStruct((PART // 12...]
    all_gather x2 -> x0, waiting for transfers between devices: 115 us -> none  [the longest x1 104 us: local(): frames = lax.all_gather(column, 'orient', axis=0, tiled=True)]
    psum x2 -> x0, blocking collectives: 48.6 us -> none  [the longest x1 35.5 us: local(): frame_total = lax.psum(jnp.sum(shifted, axis=1), 'orient')]
    pmax x1 -> x0, blocking collectives: 40.3 us -> none  [local(): frame_peak = lax.pmax(jnp.max(scores, axis=1), 'orient')]
    dot_general x2 -> x0, matrix products: 29 us -> none  [the longest x1 15.2 us: local(): lax.dot_general(prob, frames, (((0,), (0,)), ((), ())), preferred_element...]
    unnamed x1 -> x0, blocking collectives: 26.2 us -> none
    reduce_scatter x1 -> x0, waiting for transfers between devices: 24.5 us -> none  [local(): scores = lax.psum_scatter(partial, 'frame', scatter_dimension=0, tiled=True)]
    all_to_all x1 -> x0, blocking collectives: 21.4 us -> none  [local(): lax.all_to_all(own, 'frame', split_axis=1, concat_axis=0, tiled=True)]
  transfers between devices with their start and end apart: 3 -> 0, of which waited for: 3 -> 0; matrix products, arithmetic and copies ran while one was open for 3% -> 0% of each run, Pallas kernels for 0% -> 0%
where the time goes in v3:
time: 249 us
  Pallas kernels  239 us (96%)
  local copies, waits for them, and re-layouts  5.76 us (2%)
  matrix products  2.89 us (1%)
    pallas_call x1, Pallas kernels, iterate(): pl.pallas_call(iterate_kernel, out_shape=jax.ShapeDtypeStruct((PART // 12...  200 us
    pallas_call x1, Pallas kernels, scatter(): pl.pallas_call(functools.partial(scatter_kernel, q_count), out_shape=jax....  20.1 us
    pallas_call x1, Pallas kernels, reduce_blocks(): pl.pallas_call(sums_kernel, out_shape=jax.ShapeDtypeStruct((48, 128), f32...  18.1 us

profile of v3, /device:TPU:0, one launch (start us, length us, event | category | flops | bytes accessed | tf_op | source)
XLA Modules:
  0.0 248.6 jit_solution(9666433218717356681)
XLA Ops:
  0.0 0.0 copy-start
  0.0 200.4 %shard_map.55.rows_ref = f32[16,512,128]{2,1,0:T(8,128)} custom-call(s32[32,16384]{1,0:T(8,128)} %counts_ref.1, f32[1,16384]{1,0:T(1,128)} %bitcast.6, f32[512,128]{1,0:T(8,128)} %interp_ref.1, bf16[512,16384]{1,0:T(8,128)(2,1)} %slices_hbm.1), custom_call_target="tpu_custom_call" | custom-call | tf_op jit(solution)/shard_map/pallas_call | solution.py:505
  200.4 0.0 copy-done
  200.4 20.1 %shard_map.56 = f32[6144,128]{1,0:T(8,128)S(1)} custom-call(s32[1]{0:T(128)} %bitcast.block_ref, f32[16,512,128]{2,1,0:T(8,128)} %shard_map.55.rows_ref, s32[512,128]{1,0:T(8,128)S(1)} %copy-done), custom_call_target="tpu_custom_call" | custom-call | tf_op jit(solution)/shard_map/pallas_call | solution.py:554
  220.6 1.8 constant_dynamic-slice_fusion
  222.4 1.1 broadcast_in_dim.18
  223.4 1.0 dynamic-slice_divide_fusion
  224.4 1.1 div.23
  225.5 0.1 sign_compare_fusion
  225.6 0.1 ne.86
  225.8 1.1 rem.44
  226.9 2.9 %fusion = f32[128,128]{1,0:T(8,128)S(1)} fusion(f32[8192]{0:T(1024)S(1)} %broadcast_in_dim.18, s32[8192]{0:T(1024)S(1)} %get-tuple-element.8, s32[8192]{0:T(1024)S(1)} %get-tuple-element.7, s32[128]{0:T(128)S(1)} %fusion.9), kind=kOutput, calls=%fused_computation | convolution fusion | flops 1613758464 | bytes 164352 | tf_op jit(solution)/shard_map/dot_general | solution.py:586
  229.8 18.1 %shard_map.57 = f32[48,128]{1,0:T(8,128)S(1)} custom-call(f32[4,4,4,2,48,128]{5,4,3,2,1,0:T(8,128)S(1)} %bitcast.4, f32[2,4,16,128]{3,2,1,0:T(8,128)S(1)} %bitcast.5), custom_call_target="tpu_custom_call" | custom-call | tf_op jit(solution)/shard_map/pallas_call | solution.py:136
  248.0 0.6 copy.7
  (2 shorter events, 0.0 us)
Async XLA Ops:
  0.0 200.4 %copy-start = (s32[512,128]{1,0:T(8,128)S(1)}, s32[512,128]{1,0:T(8,128)}, u32[]{:S(2)}) copy-start(s32[512,128]{1,0:T(8,128)} %index_hbm.1) | copy-start | bytes 786436

commit v4 on v3

--- a/solution.py
+++ b/solution.py
@@ -145,15 +145,17 @@
 PART = 2048
 HALF = 256
 HELD = 272
+CUT = 136
 score_beta = 1.5
 NT = (((1,), (1,)), ((), ()))
 
 
-def iterate_kernel(counts_ref, gain_ref, interp_ref, slices_hbm, rows_ref,
-                   own, frames, part, stream, logs, log_mean, scores, pair_in, blocks, z1_in, kept, z2_in,
+def iterate_kernel(counts_hbm, gain_ref, interp_ref, index_ref, slices_hbm, rows_hbm, voxel_weight_ref,
+                   counts_ref, rows_ref, index_rows, weight_rows,
+                   own, frames, part, stream, logs, log_mean, scores, pair_in, blocks_a, blocks_b, z1a_in, z1b_in, kept_a, kept_b, z2a_in, z2b_in,
                    shifted, photon, stat, stat2, stat3, sib_in, x_in, y_in, prob, gathered, mass,
-                   load_sem, a2a_send, a2a_recv, g_send, g_recv, pair_sem, z1_sem, z2_sem, sib_sem,
-                   x_send, x_recv, y_send, y_recv, ag1_sem, ag2_sem, agc_sem):
+                   load_sem, rows_sem, a2a_send, a2a_recv, g_send, g_recv, pair_sem, z1a_sem, z1b_sem, z2a_sem, z2b_sem, sib_sem,
+                   x_send, x_recv, y_send, y_recv, ag_send, ag_recv, agc_sem):
     f32, b16 = jnp.float32, jnp.bfloat16
     x, y, z, core = me = here()
     plane = z * 2 + core
@@ -175,6 +177,8 @@
     def when(s, body, limit=PARTS):
         pl.when((s >= 0) & (s < limit))(lambda: body(s))
 
+    count_copy = pltpu.make_async_copy(counts_hbm, counts_ref, load_sem.at[3])
+    count_copy.start()
     load = pltpu.make_async_copy(
         slices_hbm.at[:, pl.ds(pl.multiple_of(plane * PART, PART), PART)], part, load_sem.at[0])
     load.start()
@@ -199,6 +203,7 @@
         own[j] = (counts_ref[:, lanes].astype(f32) * gain_ref[:, lanes]).astype(b16)
         return carry
 
+    count_copy.wait()
     lax.fori_loop(0, PARTS, correct, 0)
     frames[plane, x, y] = own[plane]
     pl.semaphore_wait(barrier, len(peers))
@@ -298,9 +303,18 @@
 
     lax.fori_loop(0, PARTS, spread, 0)
     mass[...] = jnp.zeros_like(mass)
+    voxel_weight_ref[...] = jnp.zeros_like(voxel_weight_ref)
+    index_rows[...] = index_ref[...].astype(f32).T
+    weight_rows[...] = weight.T
+    first_q = pl.ds(pl.multiple_of(plane * 16, 16), 16)
+    index_part, weight_part = index_rows[first_q, :], weight_rows[first_q, :]
+    for q in range(16):
+        index_rows[8 * q:8 * q + 8] = jnp.broadcast_to(index_part[q:q + 1], (8, 2 * HALF))
+        weight_rows[8 * q:8 * q + 8] = jnp.broadcast_to(weight_part[q:q + 1], (8, 2 * HALF))
 
     def clear(j, carry):
-        gathered[pl.ds(pl.multiple_of(j * 16, 16), 16), :] = jnp.zeros((16, PART), f32)
+        some = pl.ds(pl.multiple_of(j * 16, 16), 16)
+        gathered[some, :] = 0.25 * part[some, :].astype(f32)
         return carry
 
     lax.fori_loop(0, 2 * HALF // 16, clear, 0)
@@ -308,11 +322,13 @@
     def pair_copy(s):
         return remote(scores.at[s % 2, 1 - core], pair_in.at[s], pair_sem.at[0, s], pair_sem.at[1, s], sibling)
 
-    def z1_copy(s):
-        return remote(blocks.at[s % 2, 1 - group], z1_in.at[s], z1_sem.at[0, s], z1_sem.at[1, s], near)
-
-    def z2_copy(s):
-        return remote(kept.at[s % 2, 1 - spot], z2_in.at[s], z2_sem.at[0, s], z2_sem.at[1, s], far)
+    def z1_copies(s):
+        return (remote(blocks_a.at[s % 2, 1 - group], z1a_in.at[s], z1a_sem.at[0, s], z1a_sem.at[1, s], near),
+                remote(blocks_b.at[s % 2, 1 - spot], z1b_in.at[s], z1b_sem.at[0, s], z1b_sem.at[1, s], far))
+
+    def z2_copies(s):
+        return (remote(kept_a.at[s % 2, 1 - spot], z2a_in.at[s], z2a_sem.at[0, s], z2a_sem.at[1, s], far),
+                remote(kept_b.at[s % 2, 1 - z % 2], z2b_in.at[s], z2b_sem.at[0, s], z2b_sem.at[1, s], near))
 
     def sib_copy(s):
         return remote(stat.at[s % 2], sib_in.at[s], sib_sem.at[0, s], sib_sem.at[1, s], sibling)
@@ -323,13 +339,10 @@
     def y_copy(s, d):
         return remote(stat3.at[s % 2], y_in.at[s, d - 1], y_send.at[s, d - 1], y_recv.at[s, d - 1], moved(me, 1, d))
 
-    def ag1_copy(s):
+    def ag_copies(s):
         lanes = pl.ds(pl.multiple_of(z * 128, 128), 128)
-        return remote(prob.at[s, core, :, lanes], prob.at[s, core, :, lanes], ag1_sem.at[0, s], ag1_sem.at[1, s], near)
-
-    def ag2_copy(s):
-        lanes = pl.ds(pl.multiple_of(spot * 256, 256), 256)
-        return remote(prob.at[s, core, :, lanes], prob.at[s, core, :, lanes], ag2_sem.at[0, s], ag2_sem.at[1, s], far)
+        return [remote(prob.at[s, core, :, lanes], prob.at[s, core, :, lanes], ag_send.at[s, d - 1], ag_recv.at[s, d - 1],
+                       moved(me, 2, d)) for d in (1, 2, 3)]
 
     def agc_copy(s):
         return remote(prob.at[s, core], prob.at[s, core], agc_sem.at[0, s], agc_sem.at[1, s], sibling)
@@ -347,19 +360,29 @@
         lax.fori_loop(0, 2, tile, 0)
         pair_copy(s).start()
 
+    def settle(copies):
+        for copy in copies:
+            copy.wait_send()
+
     def add_pair(s):
-        pl.when(s >= 2)(lambda: z1_copy(s - 2).wait_send())
+        pl.when(s >= 2)(lambda: settle(z1_copies(s - 2)))
         pair_copy(s).wait_recv()
         for b, (g, n) in enumerate(((0, 0), (1, 0), (1, 1), (0, 1))):
             lanes = slice(128 * b, 128 * b + 128)
-            blocks[s % 2, g, n] = scores[s % 2, core, :, lanes] + pair_in[s, :, lanes]
-        z1_copy(s).start()
-
-    def add_near(s):
-        pl.when(s >= 2)(lambda: z2_copy(s - 2).wait_send())
-        z1_copy(s).wait_recv()
-        kept[s % 2] = blocks[s % 2, group] + z1_in[s]
-        z2_copy(s).start()
+            total = scores[s % 2, core, :, lanes] + pair_in[s, :, lanes]
+            blocks_a[s % 2, g, n] = total[:CUT]
+            blocks_b[s % 2, b // 2, b % 2] = total[CUT:]
+        for copy in z1_copies(s):
+            copy.start()
+
+    def add_first(s):
+        pl.when(s >= 2)(lambda: settle(z2_copies(s - 2)))
+        for copy in z1_copies(s):
+            copy.wait_recv()
+        kept_a[s % 2] = blocks_a[s % 2, group] + z1a_in[s]
+        kept_b[s % 2] = blocks_b[s % 2, spot] + z1b_in[s]
+        for copy in z2_copies(s):
+            copy.start()
 
     first_row = lax.broadcasted_iota(jnp.int32, (8, 128), 0) == 0
 
@@ -372,10 +395,13 @@
 
     def score(s):
         pl.when(s >= 2)(lambda: sib_copy(s - 2).wait_send())
-        z2_copy(s).wait_recv()
-        total = kept[s % 2, spot] + z2_in[s]
-        photons = total[HALF:HALF + 1]
-        value = (total[:HALF] - photons * log_mean[...]) * (score_beta / pixel_count)
+        for copy in z2_copies(s):
+            copy.wait_recv()
+        upper = kept_a[s % 2, spot] + z2a_in[s]
+        lower = kept_b[s % 2, z % 2] + z2b_in[s]
+        photons = lower[HALF - CUT:HALF - CUT + 1]
+        value = jnp.concatenate([upper, lower[:HALF - CUT]], axis=0)
+        value = (value - photons * log_mean[...]) * (score_beta / pixel_count)
         peak = jnp.max(value, axis=0, keepdims=True)
         value = jnp.exp(value - peak)
         shifted[s % 2] = value
@@ -384,7 +410,7 @@
         sib_copy(s).start()
 
     def add_sibling(s):
-        pl.when(s >= 2)(lambda: [x_copy(s - 2, d).wait_send() for d in (1, 2, 3)] and None)
+        pl.when(s >= 2)(lambda: settle([x_copy(s - 2, d) for d in (1, 2, 3)]))
         sib_copy(s).wait_recv()
         peak, total = combine([stat[s % 2], sib_in[s]])
         stat2[s % 2] = jnp.where(first_row, peak, total)
@@ -392,7 +418,7 @@
             x_copy(s, d).start()
 
     def add_x(s):
-        pl.when(s >= 2)(lambda: [y_copy(s - 2, d).wait_send() for d in (1, 2, 3)] and None)
+        pl.when(s >= 2)(lambda: settle([y_copy(s - 2, d) for d in (1, 2, 3)]))
         for d in (1, 2, 3):
             x_copy(s, d).wait_recv()
         peak, total = combine([stat2[s % 2], x_in[s, 0], x_in[s, 1], x_in[s, 2]])
@@ -411,14 +437,12 @@
         upper = photons.astype(b16).astype(f32)
         row = lax.broadcasted_iota(jnp.int32, (HELD - HALF, 128), 0)
         prob[s, core, HALF:, lanes] = jnp.where(row == 0, upper, jnp.where(row == 1, photons - upper, 0.0)).astype(b16)
-        ag1_copy(s).start()
-
-    def spread_near(s):
-        ag1_copy(s).wait_recv()
-        ag2_copy(s).start()
-
-    def spread_far(s):
-        ag2_copy(s).wait_recv()
+        for copy in ag_copies(s):
+            copy.start()
+
+    def share_pair(s):
+        for copy in ag_copies(s):
+            copy.wait_recv()
         agc_copy(s).start()
 
     def gather_pixels(s):
@@ -435,38 +459,55 @@
 
         lax.fori_loop(0, PARTS, tile, 0)
 
+    def weigh(t):
+        for q in (2 * t, 2 * t + 1):
+            rows = pl.ds(pl.multiple_of(q * 8, 8), 8)
+            target = index_rows[rows, :][0:1].astype(jnp.int32)
+            amount = weight_rows[rows, :][0:1]
+            owner = (target * 43691) >> 21
+            lower = target - 48 * owner
+            slot = (owner & 1) * 64 + (owner >> 1)
+            row = lax.broadcasted_iota(jnp.int32, (128, 2 * HALF), 0)
+            amount_hi = amount.astype(b16).astype(f32)
+            hot = jnp.where(row == slot, 1.0, 0.0).astype(b16)
+            parts = jnp.concatenate([jnp.where(row == lower, amount_hi, 0.0).astype(b16),
+                                     jnp.where(row == lower, amount - amount_hi, 0.0).astype(b16)], axis=0)
+            out = lax.dot_general(hot, parts, NT, preferred_element_type=f32)
+            voxel_weight_ref[...] += out[:, :128] + out[:, 128:]
+
     def tick(t, carry):
         when(t + 2, gather(3))
         when(t + 3, gather(2))
         when(t + 4, gather(1))
         when(t + 1, gather(4))
+        when(t - 2, add_pair)
+        when(t - 3, score)
+        when(t - 4, add_x)
+        when(t - 5, share_pair)
+        when(t, weigh)
         when(t, gather(5))
         when(t - 1, multiply)
-        when(t - 2, score)
-        when(t - 3, spread_near)
-        when(t - 1, add_pair)
-        when(t - 2, add_sibling)
-        when(t - 3, spread_far)
-        when(t - 2, add_x)
-        when(t - 1, add_near)
-        when(t - 2, normalise)
-        when(t - 3, gather_pixels)
-        return carry
-
-    lax.fori_loop(-1, PARTS + 3, tick, 0)
+        when(t - 2, add_first)
+        when(t - 3, add_sibling)
+        when(t - 4, normalise)
+        when(t - 5, gather_pixels)
+        return carry
+
+    lax.fori_loop(-1, PARTS + 5, tick, 0)
 
     share = 1.0 / (jnp.sum(mass[...], axis=2, keepdims=True) * (1.0 / pixel_count) + 0.25)
+    writes = []
     for q in range(PART // 128):
         for h in range(2):
             lanes, some = slice(128 * q, 128 * q + 128), slice(h * HALF, h * HALF + HALF)
-            rows_ref[q, some] = rows_ref[q, some] * (
-                (gathered[some, lanes] + 0.25 * part[some, lanes].astype(f32)) * share[h])
+            rows_ref[q, some] = rows_ref[q, some] * (gathered[some, lanes] * share[h])
+        writes.append(pltpu.make_async_copy(rows_ref.at[q], rows_hbm.at[q], rows_sem.at[q]))
+        writes[-1].start()
 
     def drain(i, carry):
         for n in range(16):
             gather_copy(i, n).wait_send()
-        ag1_copy(i).wait_send()
-        ag2_copy(i).wait_send()
+        settle(ag_copies(i))
         agc_copy(i).wait_send()
         return carry
 
@@ -479,38 +520,43 @@
     lax.fori_loop(1, PARTS, drain_a2a, 0)
     for s in (PARTS - 2, PARTS - 1):
         pair_copy(s).wait_send()
-        z1_copy(s).wait_send()
-        z2_copy(s).wait_send()
+        settle(z1_copies(s))
+        settle(z2_copies(s))
         sib_copy(s).wait_send()
         for d in (1, 2, 3):
             x_copy(s, d).wait_send()
             y_copy(s, d).wait_send()
-
-
-def iterate(counts, gain, interp, slices):
+    for write in writes:
+        write.wait()
+
+
+def iterate(counts, gain, interp, index, slices):
     f32, b16 = jnp.float32, jnp.bfloat16
     vm, dma = pltpu.VMEM, pltpu.SemaphoreType.DMA
     n = PARTS
     scratch = [
+        vm((32, n * PART), jnp.int32), vm((PART // 128, 2 * HALF, 128), f32), vm((128, 2 * HALF), f32), vm((128, 2 * HALF), f32),
         vm((n, 32, PART), b16), vm((n, 4, 4, 32, PART), b16), vm((2 * HALF, PART), b16), vm((2, HALF, PART), b16),
         vm((2, HELD, PART), b16), vm((HALF, 128), f32), vm((2, 2, HELD, 512), f32), vm((n, HELD, 512), f32),
-        vm((2, 2, 2, HELD, 128), f32), vm((n, 2, HELD, 128), f32), vm((2, 2, HELD, 128), f32), vm((n, HELD, 128), f32),
+        vm((2, 2, 2, CUT, 128), f32), vm((2, 2, 2, CUT, 128), f32), vm((n, 2, CUT, 128), f32), vm((n, 2, CUT, 128), f32),
+        vm((2, 2, CUT, 128), f32), vm((2, 2, CUT, 128), f32), vm((n, CUT, 128), f32), vm((n, CUT, 128), f32),
         vm((2, HALF, 128), f32), vm((2, 8, 128), f32), vm((2, 8, 128), f32), vm((2, 8, 128), f32), vm((2, 8, 128), f32),
         vm((n, 8, 128), f32), vm((n, 3, 8, 128), f32), vm((n, 3, 8, 128), f32),
         vm((n, 2, HELD, 512), b16), vm((2 * HALF, PART), f32), vm((2, HALF, HELD - HALF), f32),
-        dma((3,)), dma((n - 1,)), dma((n,)), dma((n, 16)), dma((n, 16)), dma((2, n)), dma((2, n)), dma((2, n)), dma((2, n)),
-        dma((n, 3)), dma((n, 3)), dma((n, 3)), dma((n, 3)), dma((2, n)), dma((2, n)), dma((2, n)),
+        dma((4,)), dma((PART // 128,)), dma((n - 1,)), dma((n,)), dma((n, 16)), dma((n, 16)),
+        dma((2, n)), dma((2, n)), dma((2, n)), dma((2, n)), dma((2, n)), dma((2, n)),
+        dma((n, 3)), dma((n, 3)), dma((n, 3)), dma((n, 3)), dma((n, 3)), dma((n, 3)), dma((2, n)),
     ]
     vspec, anyspec = pl.BlockSpec(memory_space=pltpu.VMEM), pl.BlockSpec(memory_space=pl.ANY)
     return pl.pallas_call(
         iterate_kernel,
-        out_shape=jax.ShapeDtypeStruct((PART // 128, 2 * HALF, 128), f32),
-        in_specs=[vspec, vspec, vspec, anyspec], out_specs=vspec, scratch_shapes=scratch,
+        out_shape=[jax.ShapeDtypeStruct((PART // 128, 2 * HALF, 128), f32), jax.ShapeDtypeStruct((128, 128), f32)],
+        in_specs=[anyspec, vspec, vspec, vspec, anyspec], out_specs=[anyspec, vspec], scratch_shapes=scratch,
         compiler_params=pltpu.CompilerParams(collective_id=2, has_side_effects=True, vmem_limit_bytes=62 * 2**20),
-    )(counts, gain.reshape(1, -1), interp, slices)
-
-
-def scatter_kernel(q_count, block_ref, rows_ref, index_hbm, out_ref, index_smem, sem, *accs):
+    )(counts, gain.reshape(1, -1), interp, index, slices)
+
+
+def scatter_kernel(q_count, rows_ref, index_hbm, out_ref, index_smem, sem, *accs):
     copy = pltpu.make_async_copy(index_hbm, index_smem, sem)
     copy.start()
     voxels = out_ref.shape[0]
@@ -523,7 +569,7 @@
 
     lax.fori_loop(0, voxels // 64, clear, 0)
     copy.wait()
-    base = block_ref[0] * q_count
+    base = lax.axis_index("frame") * q_count
 
     def step(t, carry):
         n = 0
@@ -549,13 +595,12 @@
     lax.fori_loop(0, voxels // 64, finish, 0)
 
 
-def scatter(rows, index, block, voxels):
+def scatter(rows, index, voxels):
     q_count = rows.shape[0]
     return pl.pallas_call(
         functools.partial(scatter_kernel, q_count),
         out_shape=jax.ShapeDtypeStruct((voxels, 128), jnp.float32),
         in_specs=[
-            pl.BlockSpec(memory_space=pltpu.SMEM),
             pl.BlockSpec(memory_space=pltpu.VMEM),
             pl.BlockSpec(memory_space=pl.ANY),
         ],
@@ -563,29 +608,13 @@
         scratch_shapes=[pltpu.SMEM(index.shape, jnp.int32), pltpu.SemaphoreType.DMA]
         + [pltpu.VMEM((voxels, 128), jnp.float32)] * ACCS,
         compiler_params=pltpu.CompilerParams(vmem_limit_bytes=48 * 2**20),
-    )(block, rows, index)
+    )(rows, index)
 
 
 def local(counts, pixel_gain, slices, voxel_index, interp):
-    frame_size = lax.axis_size("frame")
-    orient_size = lax.axis_size("orient")
-    me = lax.axis_index("frame")
-    q_count = PART // 128
-    voxels = VB_DEV * orient_size * frame_size
-    rows = iterate(counts, pixel_gain, interp, slices)
-    block = jnp.full((1,), me, jnp.int32)
-    voxel_sum = scatter(rows, voxel_index, block, voxels)
-    weight = lax.dynamic_slice_in_dim(interp, me * q_count, q_count, axis=1)
-    targets = lax.dynamic_slice_in_dim(voxel_index, me * q_count, q_count, axis=1).reshape(1, -1)
-    flat_weight = weight.reshape(1, -1)
-    upper, lower = targets // VB_DEV, targets % VB_DEV
-    slot = lax.broadcasted_iota(jnp.int32, (128, 1), 0)
-    owner = 2 * (slot % 64) + slot // 64
-    hot_upper = (upper == owner).astype(jnp.float32)
-    hot_lower = jnp.where(lower == slot, flat_weight, 0.0)
-    voxel_weight = lax.dot_general(
-        hot_upper, hot_lower, (((1,), (1,)), ((), ())), precision=lax.Precision.HIGHEST
-    )
+    voxels = VB_DEV * lax.axis_size("orient") * lax.axis_size("frame")
+    rows, voxel_weight = iterate(counts, pixel_gain, interp, voxel_index, slices)
+    voxel_sum = scatter(rows, voxel_index, voxels)
     return reduce_blocks(
         voxel_sum.reshape(SIDE, SIDE, SIDE, 2, VB_DEV, 128), voxel_weight.reshape(2, SIDE, SIDE * SIDE, 128)
     )

time: 249 us -> 208 us (0.84)
  Pallas kernels: 239 us -> 207 us
  local copies, waits for them, and re-layouts: 5.76 us -> 0.62 us
  matrix products: 2.89 us -> 0 us
    pallas_call x1, Pallas kernels: 200 us -> 168 us  [iterate(): pl.pallas_call(iterate_kernel, out_shape=[jax.ShapeDtypeStruct((PART // 1...]
    dot_general x1 -> x0, matrix products: 2.89 us -> none  [local(): lax.dot_general(hot_upper, hot_lower, (((1,), (1,)), ((), ())), precision...]
where the time goes in v4:
time: 208 us
  Pallas kernels  207 us (100%)
    pallas_call x1, Pallas kernels, iterate(): pl.pallas_call(iterate_kernel, out_shape=[jax.ShapeDtypeStruct((PART // 1...  168 us
    pallas_call x1, Pallas kernels, scatter(): pl.pallas_call(functools.partial(scatter_kernel, q_count), out_shape=jax....  20.1 us
    pallas_call x1, Pallas kernels, reduce_blocks(): pl.pallas_call(sums_kernel, out_shape=jax.ShapeDtypeStruct((48, 128), f32...  19.3 us

profile of v4, /device:TPU:0, one launch (start us, length us, event | category | flops | bytes accessed | tf_op | source)
XLA Modules:
  0.0 207.9 jit_solution(3940615879566454079)
XLA Ops:
  0.0 0.0 copy-start
  0.0 167.8 %shard_map.55 = (f32[16,512,128]{2,1,0:T(8,128)}, f32[128,128]{1,0:T(8,128)}) custom-call(s32[32,16384]{1,0:T(8,128)} %counts_hbm.1, f32[1,16384]{1,0:T(1,128)} %bitcast.5, f32[512,128]{1,0:T(8,128)} %interp_ref.1, s32[512,128]{1,0:T(8,128)} %index_hbm.1, bf16[512,16384]{1,0:T(8,128)(2,1)} %slices_hbm.1), custom_call_target="tpu_custom_call" | custom-call | tf_op jit(solution)/shard_map/pallas_call | solution.py:551
  167.8 0.0 copy-start.1
  167.8 0.0 copy-done
  167.8 20.1 %shard_map.56 = f32[6144,128]{1,0:T(8,128)S(1)} custom-call(f32[16,512,128]{2,1,0:T(8,128)} %get-tuple-element.7.rows_ref, s32[512,128]{1,0:T(8,128)S(1)} %copy-done), custom_call_target="tpu_custom_call" | custom-call | tf_op jit(solution)/shard_map/pallas_call | solution.py:600
  188.0 0.0 copy-done.1
  188.0 19.3 %shard_map.57 = f32[48,128]{1,0:T(8,128)S(1)} custom-call(f32[4,4,4,2,48,128]{5,4,3,2,1,0:T(8,128)S(1)} %bitcast.3, f32[2,4,16,128]{3,2,1,0:T(8,128)S(1)} %bitcast.4), custom_call_target="tpu_custom_call" | custom-call | tf_op jit(solution)/shard_map/pallas_call | solution.py:136
  207.3 0.6 copy.7
Async XLA Ops:
  0.0 167.8 %copy-start = (s32[512,128]{1,0:T(8,128)S(1)}, s32[512,128]{1,0:T(8,128)}, u32[]{:S(2)}) copy-start(s32[512,128]{1,0:T(8,128)} %index_hbm.1) | copy-start | bytes 786436
  167.8 20.2 %copy-start.1 = (f32[128,128]{1,0:T(8,128)S(1)}, f32[128,128]{1,0:T(8,128)}, u32[]{:S(2)}) copy-start(f32[128,128]{1,0:T(8,128)} %get-tuple-element.8) | copy-start | bytes 196612

commit v5 on v4

--- a/solution.py
+++ b/solution.py
@@ -476,19 +476,19 @@
             voxel_weight_ref[...] += out[:, :128] + out[:, 128:]
 
     def tick(t, carry):
-        when(t + 2, gather(3))
-        when(t + 3, gather(2))
-        when(t + 4, gather(1))
         when(t + 1, gather(4))
         when(t - 2, add_pair)
         when(t - 3, score)
         when(t - 4, add_x)
+        when(t + 2, gather(3))
+        when(t + 3, gather(2))
+        when(t + 4, gather(1))
         when(t - 5, share_pair)
-        when(t, weigh)
         when(t, gather(5))
+        when(t - 3, add_sibling)
         when(t - 1, multiply)
         when(t - 2, add_first)
-        when(t - 3, add_sibling)
+        when(t, weigh)
         when(t - 4, normalise)
         when(t - 5, gather_pixels)
         return carry

time: 208 us -> 206 us (level)
  no operation moved by 1% of the time
where the time goes in v5:
time: 206 us
  Pallas kernels  205 us (100%)
    pallas_call x1, Pallas kernels, iterate(): pl.pallas_call(iterate_kernel, out_shape=[jax.ShapeDtypeStruct((PART // 1...  166 us
    pallas_call x1, Pallas kernels, scatter(): pl.pallas_call(functools.partial(scatter_kernel, q_count), out_shape=jax....  20.1 us
    pallas_call x1, Pallas kernels, reduce_blocks(): pl.pallas_call(sums_kernel, out_shape=jax.ShapeDtypeStruct((48, 128), f32...  18.4 us

profile of v5, /device:TPU:0, one launch (start us, length us, event | category | flops | bytes accessed | tf_op | source)
XLA Modules:
  0.0 205.7 jit_solution(16624164815273020473)
XLA Ops:
  0.0 0.0 copy-start
  0.0 166.5 %shard_map.55 = (f32[16,512,128]{2,1,0:T(8,128)}, f32[128,128]{1,0:T(8,128)}) custom-call(s32[32,16384]{1,0:T(8,128)} %counts_hbm.1, f32[1,16384]{1,0:T(1,128)} %bitcast.5, f32[512,128]{1,0:T(8,128)} %interp_ref.1, s32[512,128]{1,0:T(8,128)} %index_hbm.1, bf16[512,16384]{1,0:T(8,128)(2,1)} %slices_hbm.1), custom_call_target="tpu_custom_call" | custom-call | tf_op jit(solution)/shard_map/pallas_call | solution.py:551
  166.5 0.0 copy-start.1
  166.5 0.0 copy-done
  166.5 20.1 %shard_map.56 = f32[6144,128]{1,0:T(8,128)S(1)} custom-call(f32[16,512,128]{2,1,0:T(8,128)} %get-tuple-element.7.rows_ref, s32[512,128]{1,0:T(8,128)S(1)} %copy-done), custom_call_target="tpu_custom_call" | custom-call | tf_op jit(solution)/shard_map/pallas_call | solution.py:600
  186.6 0.0 copy-done.1
  186.7 18.4 %shard_map.57 = f32[48,128]{1,0:T(8,128)S(1)} custom-call(f32[4,4,4,2,48,128]{5,4,3,2,1,0:T(8,128)S(1)} %bitcast.3, f32[2,4,16,128]{3,2,1,0:T(8,128)S(1)} %bitcast.4), custom_call_target="tpu_custom_call" | custom-call | tf_op jit(solution)/shard_map/pallas_call | solution.py:136
  205.1 0.6 copy.7
Async XLA Ops:
  0.0 166.5 %copy-start = (s32[512,128]{1,0:T(8,128)S(1)}, s32[512,128]{1,0:T(8,128)}, u32[]{:S(2)}) copy-start(s32[512,128]{1,0:T(8,128)} %index_hbm.1) | copy-start | bytes 786436
  166.5 20.2 %copy-start.1 = (f32[128,128]{1,0:T(8,128)S(1)}, f32[128,128]{1,0:T(8,128)}, u32[]{:S(2)}) copy-start(f32[128,128]{1,0:T(8,128)} %get-tuple-element.8) | copy-start | bytes 196612

commit v6 on v5

--- a/solution.py
+++ b/solution.py
@@ -484,11 +484,11 @@
         when(t + 3, gather(2))
         when(t + 4, gather(1))
         when(t - 5, share_pair)
+        when(t, weigh)
         when(t, gather(5))
         when(t - 3, add_sibling)
         when(t - 1, multiply)
         when(t - 2, add_first)
-        when(t, weigh)
         when(t - 4, normalise)
         when(t - 5, gather_pixels)
         return carry

time: 206 us -> 205 us (level)
  no operation moved by 1% of the time
where the time goes in v6:
time: 205 us
  Pallas kernels  204 us (100%)
    pallas_call x1, Pallas kernels, iterate(): pl.pallas_call(iterate_kernel, out_shape=[jax.ShapeDtypeStruct((PART // 1...  166 us
    pallas_call x1, Pallas kernels, scatter(): pl.pallas_call(functools.partial(scatter_kernel, q_count), out_shape=jax....  20.1 us
    pallas_call x1, Pallas kernels, reduce_blocks(): pl.pallas_call(sums_kernel, out_shape=jax.ShapeDtypeStruct((48, 128), f32...  18.3 us

profile of v6, /device:TPU:0, one launch (start us, length us, event | category | flops | bytes accessed | tf_op | source)
XLA Modules:
  0.0 205.1 jit_solution(12910482460702112596)
XLA Ops:
  0.0 0.0 copy-start
  0.0 166.0 %shard_map.55 = (f32[16,512,128]{2,1,0:T(8,128)}, f32[128,128]{1,0:T(8,128)}) custom-call(s32[32,16384]{1,0:T(8,128)} %counts_hbm.1, f32[1,16384]{1,0:T(1,128)} %bitcast.5, f32[512,128]{1,0:T(8,128)} %interp_ref.1, s32[512,128]{1,0:T(8,128)} %index_hbm.1, bf16[512,16384]{1,0:T(8,128)(2,1)} %slices_hbm.1), custom_call_target="tpu_custom_call" | custom-call | tf_op jit(solution)/shard_map/pallas_call | solution.py:551
  166.0 0.0 copy-start.1
  166.0 0.0 copy-done
  166.0 20.1 %shard_map.56 = f32[6144,128]{1,0:T(8,128)S(1)} custom-call(f32[16,512,128]{2,1,0:T(8,128)} %get-tuple-element.7.rows_ref, s32[512,128]{1,0:T(8,128)S(1)} %copy-done), custom_call_target="tpu_custom_call" | custom-call | tf_op jit(solution)/shard_map/pallas_call | solution.py:600
  186.2 0.0 copy-done.1
  186.2 18.3 %shard_map.57 = f32[48,128]{1,0:T(8,128)S(1)} custom-call(f32[4,4,4,2,48,128]{5,4,3,2,1,0:T(8,128)S(1)} %bitcast.3, f32[2,4,16,128]{3,2,1,0:T(8,128)S(1)} %bitcast.4), custom_call_target="tpu_custom_call" | custom-call | tf_op jit(solution)/shard_map/pallas_call | solution.py:136
  204.5 0.6 copy.7
Async XLA Ops:
  0.0 166.0 %copy-start = (s32[512,128]{1,0:T(8,128)S(1)}, s32[512,128]{1,0:T(8,128)}, u32[]{:S(2)}) copy-start(s32[512,128]{1,0:T(8,128)} %index_hbm.1) | copy-start | bytes 786436
  166.0 20.2 %copy-start.1 = (f32[128,128]{1,0:T(8,128)S(1)}, f32[128,128]{1,0:T(8,128)}, u32[]{:S(2)}) copy-start(f32[128,128]{1,0:T(8,128)} %get-tuple-element.8) | copy-start | bytes 196612
